TPU v7x, 256 devices: a whole 4x4x8 slice. The times are simulated.
256 devices in a mesh: row: 32 (over y_lo, z, core), col: 8 (over x, y_hi).
Axes of the slice: x: 4, y: 4 (y_hi: 2, y_lo: 2; y = y_hi * 2 + y_lo), z: 8, core: 2. Of those that a mesh axis runs over, the one named last changes fastest.
Arguments:
- start_block: float32 [32768, 256], P(('row', 'col')), may hold values from -6 to 6
- tiles: bfloat16 [32, 8, 14, 128, 128], P('row', 'col'), may hold values from -0.125 to 0.125
- tile_rows: int32 [32, 8, 14], P('row', 'col'), may hold values from -1 to 255, as said below
- tile_cols: int32 [32, 8, 14], P('row', 'col'), may hold values from -1 to 255, as said below
- bounds: float32 [3], replicated, may hold values from -2.6 to 2.6, as said below
Outputs:
- filtered: float32 [32768, 256], P(('row', 'col'))
Inputs may be any that keep to these rules, and one draw needn't show every extreme that they name: Vector rows form blocks of 128 rows, one block a device, in row+col order. On the device at grid row r and grid column c, a live slot names a block row held by one of the devices (r, any column) and a block column held by one of the devices (any row, c). Live slots come first; each device has 1 to 14 live slots, and one device has exactly 14 in every draw. No block position is named twice, and the mirror of a named position is never named unless it lies on the diagonal. tile_rows and tile_cols are -1 together. `tile_cols`: same slots as tile_rows. bounds[0] < bounds[1] < bounds[2].
All inputs are finite; a program needn't handle non-finite values.
Results may differ from a plain program's by a relative error of at most 0.0042.
Values may be sent and summed in bfloat16 or wider, within the bound.
No kernel may reach another device: no remote copies, remote signals or barrier semaphores. Data moves between devices by JAX's collectives and lax.ppermute only.
A program may use at most 64 MiB of HBM per device.

v0:
```python
import jax
import jax.numpy as jnp
from jax import lax
from jax.sharding import PartitionSpec as P

DEGREE = 4


def local(start_block, tiles, tile_rows, tile_cols, bounds):
    rows_dev, vec_width = start_block.shape
    tile_size = tiles.shape[-1]
    blocks = rows_dev // tile_size
    row_count = lax.axis_size("row")
    col_count = lax.axis_size("col")
    near_count = col_count * blocks
    far_count = row_count * blocks
    row_index = lax.axis_index("row")
    slots = tiles.shape[2]
    tile_mats = tiles.reshape(slots, tile_size, tile_size)
    glob_rows = tile_rows.reshape(slots)
    glob_cols = tile_cols.reshape(slots)
    is_live = glob_rows >= 0
    local_rows = jnp.where(is_live, glob_rows - row_index * near_count, -1)
    local_cols = jnp.where(
        is_live, glob_cols // blocks // col_count * blocks + glob_cols % blocks, -1
    )
    row_table = (local_rows[None, :] == lax.iota(jnp.int32, near_count)[:, None]).astype(
        jnp.float32
    )
    col_table = (local_cols[None, :] == lax.iota(jnp.int32, far_count)[:, None]).astype(jnp.float32)
    rows_safe = jnp.maximum(local_rows, 0)
    cols_safe = jnp.maximum(local_cols, 0)

    def apply_matrix(vectors):
        low_vectors = vectors.astype(jnp.bfloat16)
        far_vectors = lax.all_gather(low_vectors, "row", axis=0, tiled=True).reshape(
            far_count, tile_size, vec_width
        )
        near_vectors = lax.all_gather(low_vectors, "col", axis=0, tiled=True).reshape(
            near_count, tile_size, vec_width
        )
        picked_far = jnp.take(far_vectors, cols_safe, axis=0)
        picked_near = jnp.take(near_vectors, rows_safe, axis=0)
        forward = jnp.einsum(
            "txy,tyk->txk", tile_mats, picked_far, preferred_element_type=jnp.float32
        )
        backward = jnp.einsum(
            "tyx,tyk->txk", tile_mats, picked_near, preferred_element_type=jnp.float32
        )
        near_partial = jnp.dot(
            row_table, forward.reshape(slots, -1), precision=lax.Precision.HIGHEST
        )
        far_partial = jnp.dot(
            col_table, backward.reshape(slots, -1), precision=lax.Precision.HIGHEST
        )
        mirrored = lax.psum_scatter(
            far_partial.reshape(far_count * tile_size, vec_width),
            "row",
            scatter_dimension=0,
            tiled=True,
        )
        combined = lax.psum_scatter(
            near_partial.reshape(near_count * tile_size, vec_width),
            "col",
            scatter_dimension=0,
            tiled=True,
        )
        return combined + mirrored

    half_width = (bounds[2] - bounds[1]) * 0.5
    center = (bounds[2] + bounds[1]) * 0.5
    sigma_one = half_width / (bounds[0] - center)
    previous = start_block
    current = (apply_matrix(start_block) - center * start_block) * (sigma_one / half_width)
    sigma = sigma_one
    for turn_index in range(DEGREE - 1):
        sigma_next = 1.0 / (2.0 / sigma_one - sigma)
        product = apply_matrix(current)
        following = (product - center * current) * (
            2.0 * sigma_next / half_width
        ) - sigma * sigma_next * previous
        previous = current
        current = following
        sigma = sigma_next
    return current


def solution(mesh):
    placed = (
        P(("row", "col"), None),
        P("row", "col", None, None, None),
        P("row", "col", None),
        P("row", "col", None),
        P(),
    )
    return jax.shard_map(
        local, mesh=mesh, in_specs=placed, out_specs=P(("row", "col"), None), check_vma=False
    )
```

profile of v0, /device:TPU:1, one launch (start us, length us, event | category | flops | bytes accessed | tf_op | source)
XLA Modules:
  0.0 1112.4 jit_solution(15374100512210820898)
XLA Ops:
  8.9 69.2 %all-gather.5.cloned.1.call-done = bf16[4096,256]{1,0:T(8,128)(2,1)} async-done(((bf16[128,256]{1,0:T(8,128)(2,1)}), bf16[4096,256]{1,0:T(8,128)(2,1)}) %all-gather.5.cloned.1.call-update) | async-done | bytes 2097168 | tf_op jit(solution)/shard_map/all_gather | solution.py:36
  78.1 2.2 gather_fusion
  80.9 1.7 copy.7
  82.6 1.7 pad.8
  87.7 29.2 %all_gather.25 = bf16[1024,256]{1,0:T(8,128)(2,1)S(1)} all-gather(bf16[128,256]{1,0:T(8,128)(2,1)S(1)} %copy-done.3), channel_id=1, replica_groups=mesh['row'=32,'col'=8] {'col'}, dimensions={0}, use_global_device_ids=true | all-gather | bytes 589824 | tf_op jit(solution)/shard_map/all_gather | solution.py:39
  118.0 1.7 copy.9
  119.8 1.7 pad.9
  122.7 3.8 fusion.35
  126.5 4.9 reshape.150
  135.8 26.8 %reduce-scatter.9.cloned.1.call-done = f32[128,256]{1,0:T(8,128)} async-done(((f32[1024,256]{1,0:T(8,128)}), f32[128,256]{1,0:T(8,128)}) %reduce-scatter.9.cloned.1.call-update) | async-done | bytes 131088 | tf_op jit(solution)/shard_map/reduce_scatter | solution.py:62
  162.6 122.1 %reduce-scatter.11.cloned.1.call-done = f32[128,256]{1,0:T(8,128)} async-done(((f32[4096,256]{1,0:T(8,128)}), f32[128,256]{1,0:T(8,128)}) %reduce-scatter.11.cloned.1.call-update) | async-done | bytes 131088 | tf_op jit(solution)/shard_map/reduce_scatter | solution.py:56
  284.7 1.6 fusion.58
  286.4 65.0 %all-gather.7.cloned.1.call-done = bf16[4096,256]{1,0:T(8,128)(2,1)} async-done(((bf16[128,256]{1,0:T(8,128)(2,1)}), bf16[4096,256]{1,0:T(8,128)(2,1)}) %all-gather.7.cloned.1.call-update) | async-done | bytes 2097168 | tf_op jit(solution)/shard_map/all_gather | solution.py:36
  351.3 2.2 gather_fusion.2
  354.1 1.7 copy.11
  355.8 1.7 pad.10
  360.9 29.3 %all_gather.27 = bf16[1024,256]{1,0:T(8,128)(2,1)S(1)} all-gather(bf16[128,256]{1,0:T(8,128)(2,1)S(1)} %copy-done.6), channel_id=1, replica_groups=mesh['row'=32,'col'=8] {'col'}, dimensions={0}, use_global_device_ids=true | all-gather | bytes 589824 | tf_op jit(solution)/shard_map/all_gather | solution.py:39
  391.3 1.7 copy.13
  393.0 1.7 pad.11
  395.9 3.8 fusion.34
  399.7 4.9 reshape.156
  404.9 31.0 %reduce-scatter.13.cloned.1.call-done = f32[128,256]{1,0:T(8,128)} async-done(((f32[1024,256]{1,0:T(8,128)}), f32[128,256]{1,0:T(8,128)}) %reduce-scatter.13.cloned.1.call-update) | async-done | bytes 131088 | tf_op jit(solution)/shard_map/reduce_scatter | solution.py:62
  435.9 121.8 %reduce-scatter.15.cloned.1.call-done = f32[128,256]{1,0:T(8,128)} async-done(((f32[4096,256]{1,0:T(8,128)}), f32[128,256]{1,0:T(8,128)}) %reduce-scatter.15.cloned.1.call-update) | async-done | bytes 131088 | tf_op jit(solution)/shard_map/reduce_scatter | solution.py:56
  557.7 1.6 fusion.57
  559.4 65.0 %all-gather.9.cloned.1.call-done = bf16[4096,256]{1,0:T(8,128)(2,1)} async-done(((bf16[128,256]{1,0:T(8,128)(2,1)}), bf16[4096,256]{1,0:T(8,128)(2,1)}) %all-gather.9.cloned.1.call-update) | async-done | bytes 2097168 | tf_op jit(solution)/shard_map/all_gather | solution.py:36
  624.4 2.2 gather_fusion.4
  627.1 1.7 copy.15
  628.8 1.7 pad.12
  633.9 29.3 %all_gather.29 = bf16[1024,256]{1,0:T(8,128)(2,1)S(1)} all-gather(bf16[128,256]{1,0:T(8,128)(2,1)S(1)} %copy-done.5), channel_id=1, replica_groups=mesh['row'=32,'col'=8] {'col'}, dimensions={0}, use_global_device_ids=true | all-gather | bytes 589824 | tf_op jit(solution)/shard_map/all_gather | solution.py:39
  664.4 1.7 copy.17
  666.1 1.7 pad.13
  669.0 3.8 fusion.33
  672.9 4.9 reshape.162
  677.9 31.0 %reduce-scatter.17.cloned.1.call-done = f32[128,256]{1,0:T(8,128)} async-done(((f32[1024,256]{1,0:T(8,128)}), f32[128,256]{1,0:T(8,128)}) %reduce-scatter.17.cloned.1.call-update) | async-done | bytes 131088 | tf_op jit(solution)/shard_map/reduce_scatter | solution.py:62
  708.9 122.0 %reduce-scatter.19.cloned.1.call-done = f32[128,256]{1,0:T(8,128)} async-done(((f32[4096,256]{1,0:T(8,128)}), f32[128,256]{1,0:T(8,128)}) %reduce-scatter.19.cloned.1.call-update) | async-done | bytes 131088 | tf_op jit(solution)/shard_map/reduce_scatter | solution.py:56
  831.0 1.7 fusion.56
  832.7 65.0 %all-gather.11.cloned.1.call-done = bf16[4096,256]{1,0:T(8,128)(2,1)} async-done(((bf16[128,256]{1,0:T(8,128)(2,1)}), bf16[4096,256]{1,0:T(8,128)(2,1)}) %all-gather.11.cloned.1.call-update) | async-done | bytes 2097168 | tf_op jit(solution)/shard_map/all_gather | solution.py:36
  897.7 2.2 gather_fusion.6
  900.4 1.7 copy.19
  902.1 1.7 pad.14
  907.2 29.3 %all_gather.31 = bf16[1024,256]{1,0:T(8,128)(2,1)S(1)} all-gather(bf16[128,256]{1,0:T(8,128)(2,1)S(1)} %copy-done.4), channel_id=1, replica_groups=mesh['row'=32,'col'=8] {'col'}, dimensions={0}, use_global_device_ids=true | all-gather | bytes 589824 | tf_op jit(solution)/shard_map/all_gather | solution.py:39
  937.7 1.7 copy.21
  939.4 1.7 pad.15
  942.4 3.8 fusion.32
  946.2 4.9 reshape.168
  951.2 31.0 %reduce-scatter.21.cloned.1.call-done = f32[128,256]{1,0:T(8,128)} async-done(((f32[1024,256]{1,0:T(8,128)}), f32[128,256]{1,0:T(8,128)}) %reduce-scatter.21.cloned.1.call-update) | async-done | bytes 131088 | tf_op jit(solution)/shard_map/reduce_scatter | solution.py:62
  982.1 121.8 %reduce-scatter.23.cloned.1.call-done = f32[128,256]{1,0:T(8,128)} async-done(((f32[4096,256]{1,0:T(8,128)}), f32[128,256]{1,0:T(8,128)}) %reduce-scatter.23.cloned.1.call-update) | async-done | bytes 131088 | tf_op jit(solution)/shard_map/reduce_scatter | solution.py:56
  1103.9 1.7 multiply_subtract_fusion
  (77 shorter events, 28.7 us)
Async XLA Ops:
  6.5 73.8 %copy-start = (bf16[1,1,14,128,128]{4,3,2,1,0:T(8,128)(2,1)S(1)}, bf16[1,1,14,128,128]{4,3,2,1,0:T(8,128)(2,1)}, u32[]{:S(2)}) copy-start(bf16[1,1,14,128,128]{4,3,2,1,0:T(8,128)(2,1)} %param.10) | copy-start | bytes 1376260
  6.5 71.6 %all-gather.5.cloned.1.call-start = ((), (), s32[]{:S(2)}) async-start(), calls=%async_computation.8 | async-start | bytes 2162688 | tf_op jit(solution)/shard_map/all_gather | solution.py:36
  8.2 154.4 %reduce-scatter.9.cloned.1.call-start = ((), (), s32[]{:S(2)}) async-start(), calls=%async_computation.9 | async-start | bytes 1179648 | tf_op jit(solution)/shard_map/reduce_scatter | solution.py:62
  86.4 1.3 copy-start.3
  87.6 197.0 %reduce-scatter.11.cloned.1.call-start = ((), (), s32[]{:S(2)}) async-start(), calls=%async_computation.10 | async-start | bytes 4325376 | tf_op jit(solution)/shard_map/reduce_scatter | solution.py:56
  131.4 0.7 copy-start.8
  131.4 153.3 %copy-start.1 = (f32[128,256]{1,0:T(8,128)S(1)}, f32[128,256]{1,0:T(8,128)}, u32[]{:S(2)}) copy-start(f32[128,256]{1,0:T(8,128)} %param.9) | copy-start | bytes 393220
  131.4 219.9 %all-gather.7.cloned.1.call-start = ((), (), s32[]{:S(2)}) async-start(), calls=%async_computation.11 | async-start | bytes 2162688 | tf_op jit(solution)/shard_map/all_gather | solution.py:36
  286.3 149.6 %reduce-scatter.13.cloned.1.call-start = ((), (), s32[]{:S(2)}) async-start(), calls=%async_computation.12 | async-start | bytes 1179648 | tf_op jit(solution)/shard_map/reduce_scatter | solution.py:62
  359.5 1.3 copy-start.6
  360.8 196.8 %reduce-scatter.15.cloned.1.call-start = ((), (), s32[]{:S(2)}) async-start(), calls=%async_computation.13 | async-start | bytes 4325376 | tf_op jit(solution)/shard_map/reduce_scatter | solution.py:56
  404.6 153.0 %copy-start.2 = (f32[128,256]{1,0:T(8,128)S(1)}, f32[128,256]{1,0:T(8,128)}, u32[]{:S(2)}) copy-start(f32[128,256]{1,0:T(8,128)} %param.9) | copy-start | bytes 393220
  404.7 219.7 %all-gather.9.cloned.1.call-start = ((), (), s32[]{:S(2)}) async-start(), calls=%async_computation.14 | async-start | bytes 2162688 | tf_op jit(solution)/shard_map/all_gather | solution.py:36
  559.3 149.6 %reduce-scatter.17.cloned.1.call-start = ((), (), s32[]{:S(2)}) async-start(), calls=%async_computation.15 | async-start | bytes 1179648 | tf_op jit(solution)/shard_map/reduce_scatter | solution.py:62
  632.6 1.3 copy-start.5
  633.8 197.1 %reduce-scatter.19.cloned.1.call-start = ((), (), s32[]{:S(2)}) async-start(), calls=%async_computation.16 | async-start | bytes 4325376 | tf_op jit(solution)/shard_map/reduce_scatter | solution.py:56
  677.8 219.9 %all-gather.11.cloned.1.call-start = ((), (), s32[]{:S(2)}) async-start(), calls=%async_computation.17 | async-start | bytes 2162688 | tf_op jit(solution)/shard_map/all_gather | solution.py:36
  832.7 149.5 %reduce-scatter.21.cloned.1.call-start = ((), (), s32[]{:S(2)}) async-start(), calls=%async_computation.18 | async-start | bytes 1179648 | tf_op jit(solution)/shard_map/reduce_scatter | solution.py:62
  905.9 1.3 copy-start.4
  907.2 196.8 %reduce-scatter.23.cloned.1.call-start = ((), (), s32[]{:S(2)}) async-start(), calls=%async_computation.19 | async-start | bytes 4325376 | tf_op jit(solution)/shard_map/reduce_scatter | solution.py:56
  951.1 152.9 %copy-start.7 = (f32[128,256]{1,0:T(8,128)S(1)}, f32[128,256]{1,0:T(8,128)}, u32[]{:S(2)}) copy-start(f32[128,256]{1,0:T(8,128)} %get-tuple-element.8) | copy-start | bytes 393220
Sparse Core Ops, SparseCore 0:
  9.2 68.8 all-gather.4
  87.7 74.7 reduce-scatter.8
  165.3 119.3 reduce-scatter.10
  286.5 64.7 all-gather.6
  360.9 74.8 reduce-scatter.12
  438.3 119.3 reduce-scatter.14
  559.5 64.8 all-gather.8
  634.0 74.9 reduce-scatter.16
  711.6 119.2 reduce-scatter.18
  832.8 64.8 all-gather.10
  907.3 74.8 reduce-scatter.20
  984.5 119.3 reduce-scatter.22
where the time goes:
time: 1120 us; the launch traced here: 1110 us
  waiting for transfers between devices  872 us (78%)
  blocking collectives  117 us (10%)
  local copies, waits for them, and re-layouts  74.2 us (7%)
  matrix products  22.6 us (2%)
  between operations  17.4 us (2%)
    reduce_scatter x4, waiting for transfers between devices, apply_matrix(): lax.psum_scatter(far_partial.reshape(far_count * tile_size, vec_width), '...  488 us
    all_gather x4, waiting for transfers between devices, apply_matrix(): lax.all_gather(low_vectors, 'row', axis=0, tiled=True)  264 us
    reduce_scatter x4, waiting for transfers between devices, apply_matrix(): lax.psum_scatter(near_partial.reshape(near_count * tile_size, vec_width),...  120 us
    all_gather x4, blocking collectives, apply_matrix(): lax.all_gather(low_vectors, 'col', axis=0, tiled=True)  117 us
    unnamed x34, local copies, waits for them, and re-layouts  24.1 us
  transfers between devices with their start and end apart: 12, of which 12 were waited for; matrix products, arithmetic and copies ran while one was open for 5% of the time, Pallas kernels for 0%

commit v1 on v0

v1 whole, which is shorter than its diff:
```python
import functools

import jax
import jax.numpy as jnp
from jax import lax
from jax.experimental import pallas as pl
from jax.experimental.pallas import tpu as pltpu
from jax.sharding import Mesh
from jax.sharding import PartitionSpec as P

DEGREE = 4
BATCH = 8
SIZES = {"yl": 2, "zh": 4, "zl": 2, "core": 2, "x": 4, "yh": 2}
GROUP = ("yl", "yh", "zl")
CHIPS = 8
BLOCKS = 2 * CHIPS
RING = 4
SUMS = RING * BLOCKS
LIST = 256


def shift_y(array, step):
    pairs = []
    for low in range(2):
        for high in range(2):
            target = (high * 2 + low - step) % 4
            pairs.append((low * 2 + high, target % 2 * 2 + target // 2))
    return lax.ppermute(array, ("yl", "yh"), pairs)


def swap(array, axis):
    return lax.ppermute(array, axis, [(0, 1), (1, 0)])


def exchange(array, step, x_core):
    pairs = []
    for high in range(RING):
        for core in range(2):
            for place in range(RING):
                if core == x_core:
                    target = (high * 2 + core) * RING + (place + step) % RING
                else:
                    target = ((high + step) % RING * 2 + core) * RING + place
                pairs.append(((high * 2 + core) * RING + place, target))
    return lax.ppermute(array, ("zh", "core", "x"), pairs)


def list_kernel(slots, meta, where, jobs, count):
    core, high, place, along_y, low = (where[i] for i in range(5))

    def source(piece, found):
        core_s = core ^ (piece >> 3)
        low_s = low ^ ((piece >> 2) & 1)
        y_s = (along_y + (piece & 3)) & 3
        block_s = core_s * 8 + ((y_s & 1) * 2 + (y_s >> 1)) * 2 + low_s

        def slot(t, found):
            row = meta[block_s * 2 * slots + t]
            col = meta[(block_s * 2 + 1) * slots + t]
            spots = []
            for number in (row, col):
                group, member = number >> 3, number & 7
                block = (
                    (group & 1) * 8
                    + ((group >> 4) * 2 + (member & 1)) * 2
                    + ((group >> 1) & 1)
                )
                spots.append((block, (group >> 2) & 3, member >> 1))
            near = ((spots[0][2] - place) & 3) * BLOCKS + spots[0][0]
            far = ((spots[1][1] - high) & 3) * BLOCKS + spots[1][0]
            taken = jnp.where(core == 0, near, far)
            given = jnp.where(core == 0, far, near)
            jobs[found] = ((piece * slots + t) << 16) | (taken << 8) | given
            return found + jnp.where(row >= 0, 1, 0)

        return lax.fori_loop(0, slots, slot, found)

    found = lax.fori_loop(0, BLOCKS, source, jnp.int32(0))
    for extra in range(BATCH):
        jobs[found + extra] = SUMS
    count[0] = (found + BATCH - 1) // BATCH


def apply_kernel(jobs, count, where, tiles, *refs):
    taken = refs[:RING]
    given = refs[RING : 2 * RING]
    vectors, sums = refs[2 * RING :]
    for d in range(RING):
        vectors[d * BLOCKS : (d + 1) * BLOCKS] = taken[d][...]
    sums[...] = jnp.zeros_like(sums)

    def multiply(contract):
        def batch(step, carry):
            products = []
            for k in range(BATCH):
                job = jobs[step * BATCH + k]
                products.append(
                    (
                        job & 255,
                        lax.dot_general(
                            vectors[(job >> 8) & 255],
                            tiles[job >> 16],
                            (((1,), (contract,)), ((), ())),
                            preferred_element_type=jnp.float32,
                        ),
                    )
                )
            for spot, product in products:
                sums[spot] += product
            return carry

        lax.fori_loop(0, count[0], batch, 0)

    @pl.when(where[0] == 0)
    def _():
        multiply(0)

    @pl.when(where[0] != 0)
    def _():
        multiply(1)

    for d in range(RING):
        given[d][...] = sums[d * BLOCKS : (d + 1) * BLOCKS].astype(given[d].dtype)


def local(start_block, tiles, tile_rows, tile_cols, bounds):
    size, width = start_block.shape
    slots = tiles.shape[2]
    part = width // CHIPS
    spot = {name: lax.axis_index(name) for name in SIZES}
    core = spot["core"]
    where = jnp.stack(
        [core, spot["zh"], spot["x"], spot["yh"] * 2 + spot["yl"], spot["zl"]]
    ).astype(jnp.int32)

    own_tiles = tiles.reshape(slots, size, size)
    places = jnp.concatenate(
        [tile_rows.reshape(1, slots), tile_cols.reshape(1, slots)]
    ).astype(jnp.float32)
    places = jnp.pad(places, ((0, 6), (0, size - slots)))
    message = jnp.concatenate(
        [
            start_block.T.reshape(CHIPS, part, size),
            jnp.broadcast_to(places[None], (CHIPS, 8, size)),
        ],
        axis=1,
    )
    mine = lax.all_to_all(message, GROUP, 0, 0)
    theirs = swap(mine, "core")
    first = jnp.where(core == 0, mine, theirs)
    second = jnp.where(core == 0, theirs, mine)
    dealt = jnp.concatenate([first, second])
    start = dealt[:, :part]
    meta = dealt[:, part : part + 2, :slots].astype(jnp.int32).reshape(-1)

    half = slots // 2
    beside = swap(own_tiles, "zl")
    up, down = shift_y(own_tiles, 1), shift_y(own_tiles, -1)
    beside_up, beside_down = shift_y(beside, 1), shift_y(beside, -1)
    over = shift_y(up[:half], 1), shift_y(down[half:], -1)
    beside_over = swap(over[0], "zl"), swap(over[1], "zl")
    pieces = [own_tiles, up, *over, down, beside, beside_up, *beside_over, beside_down]
    all_tiles = jnp.concatenate(pieces + [swap(piece, "core") for piece in pieces])

    smem = pl.BlockSpec(memory_space=pltpu.SMEM)
    vmem = pl.BlockSpec(memory_space=pltpu.VMEM)
    jobs, count = pl.pallas_call(
        functools.partial(list_kernel, slots),
        out_shape=(
            jax.ShapeDtypeStruct((LIST,), jnp.int32),
            jax.ShapeDtypeStruct((1,), jnp.int32),
        ),
        in_specs=[smem, smem],
        out_specs=(smem, smem),
        name="list_jobs",
    )(meta, where)
    apply_tiles = pl.pallas_call(
        apply_kernel,
        out_shape=[jax.ShapeDtypeStruct((BLOCKS, part, size), jnp.float32)]
        + [jax.ShapeDtypeStruct((BLOCKS, part, size), jnp.bfloat16)] * (RING - 1),
        in_specs=[smem, smem, smem] + [vmem] * (1 + RING),
        out_specs=[vmem] * RING,
        scratch_shapes=[
            pltpu.VMEM((SUMS, part, size), jnp.bfloat16),
            pltpu.VMEM((SUMS + 1, part, size), jnp.float32),
        ],
        compiler_params=pltpu.CompilerParams(vmem_limit_bytes=32 << 20),
        name="apply_tiles",
    )

    def apply_matrix(vectors):
        low = vectors.astype(jnp.bfloat16)
        gathered = {d: exchange(low, -d, 0) for d in (2, 1, 3)}
        total, *partial = apply_tiles(
            jobs, count, where, all_tiles, low, *(gathered[d] for d in (1, 2, 3))
        )
        sent = [exchange(partial[d - 1], d, 1) for d in (2, 1, 3)]
        for piece in sent:
            total = total + piece.astype(jnp.float32)
        return total + swap(total, "core")

    half_width = (bounds[2] - bounds[1]) * 0.5
    center = (bounds[2] + bounds[1]) * 0.5
    sigma_one = half_width / (bounds[0] - center)
    previous = start
    current = (apply_matrix(start) - center * start) * (sigma_one / half_width)
    sigma = sigma_one
    for _ in range(DEGREE - 1):
        sigma_next = 1.0 / (2.0 / sigma_one - sigma)
        product = apply_matrix(current)
        following = (product - center * current) * (2.0 * sigma_next / half_width) - (
            sigma * sigma_next
        ) * previous
        previous = current
        current = following
        sigma = sigma_next
    keep = jnp.where(core == 0, current[:CHIPS], current[CHIPS:])
    back = lax.all_to_all(keep, GROUP, 0, 0)
    return back.reshape(width, size).T


def solution(mesh):
    fine = Mesh(mesh.devices.reshape(tuple(SIZES.values())), tuple(SIZES))
    row, col = ("yl", "zh", "zl", "core"), ("x", "yh")
    placed = (
        P(row + col, None),
        P(row, col, None, None, None),
        P(row, col, None),
        P(row, col, None),
        P(),
    )
    return jax.shard_map(
        local, mesh=fine, in_specs=placed, out_specs=P(row + col, None), check_vma=False
    )
```

time: 1120 us -> 203 us (0.18)
  waiting for transfers between devices: 872 us -> 52.9 us
  blocking collectives: 117 us -> 8.97 us
  starting transfers between devices: 0.46 us -> 76.4 us
  local copies, waits for them, and re-layouts: 74.2 us -> 32.6 us
  Pallas kernels: 0 us -> 26 us
  matrix products: 22.6 us -> 0 us
  between operations: 17.4 us -> 3.88 us
    reduce_scatter x8 -> x0, waiting for transfers between devices: 608 us -> none  [the longest x4 488 us: apply_matrix(): lax.psum_scatter(far_partial.reshape(far_count * tile_size, vec_width), '...]
    all_gather x4 -> x0, waiting for transfers between devices: 264 us -> none  [apply_matrix(): lax.all_gather(low_vectors, 'row', axis=0, tiled=True)]
    all_gather x4 -> x0, blocking collectives: 117 us -> none  [apply_matrix(): lax.all_gather(low_vectors, 'col', axis=0, tiled=True)]
    ppermute x0 -> x48, starting transfers between devices: none -> 70 us  [the longest x24 43.5 us: exchange(): return lax.ppermute(array, ('zh', 'core', 'x'), pairs)]
    ppermute x0 -> x48, waiting for transfers between devices: none -> 52.7 us  [the longest x24 37.1 us: exchange(): return lax.ppermute(array, ('zh', 'core', 'x'), pairs)]
    pallas_call x0 -> x5, Pallas kernels: none -> 26 us  [the longest x4 19.4 us: apply_matrix(): apply_tiles(jobs, count, where, all_tiles, low, *(gathered[d] for d in (1...]
    reshape x8 -> x2, local copies, waits for them, and re-layouts: 24.5 us -> 1.45 us  [the longest x1 0.76 us: local(): return back.reshape(width, size).T]
    dot_general x16 -> x0, matrix products: 22.6 us -> none  [the longest x4 15.2 us: apply_matrix(): jnp.dot(col_table, backward.reshape(slots, -1), precision=lax.Precision.H...]
  transfers between devices with their start and end apart: 12 -> 49, of which waited for: 12 -> 27; matrix products, arithmetic and copies ran while one was open for 5% -> 9% of each run, Pallas kernels for 0% -> 3%
where the time goes in v1:
time: 203 us
  starting transfers between devices  76.4 us (38%)
  waiting for transfers between devices  52.9 us (26%)
  local copies, waits for them, and re-layouts  32.6 us (16%)
  Pallas kernels  26 us (13%)
  blocking collectives  8.97 us (4%)
  between operations  3.88 us (2%)
    ppermute x24, starting transfers between devices, exchange(): return lax.ppermute(array, ('zh', 'core', 'x'), pairs)  43.5 us
    ppermute x24, waiting for transfers between devices, exchange(): return lax.ppermute(array, ('zh', 'core', 'x'), pairs)  37.1 us
    unnamed x33, local copies, waits for them, and re-layouts  28 us
    pallas_call x4, Pallas kernels, apply_matrix(): apply_tiles(jobs, count, where, all_tiles, low, *(gathered[d] for d in (1...  19.4 us
    ppermute x18, starting transfers between devices, swap(): return lax.ppermute(array, axis, [(0, 1), (1, 0)])  17.9 us
    all_to_all x1, blocking collectives, local(): back = lax.all_to_all(keep, GROUP, 0, 0)  8.97 us
    ppermute x6, starting transfers between devices, shift_y(): return lax.ppermute(array, ('yl', 'yh'), pairs)  8.67 us
    ppermute x18, waiting for transfers between devices, swap(): return lax.ppermute(array, axis, [(0, 1), (1, 0)])  7.82 us
  transfers between devices with their start and end apart: 49, of which 27 were waited for; matrix products, arithmetic and copies ran while one was open for 9% of the time, Pallas kernels for 3%

profile of v1, /device:TPU:1, one launch (start us, length us, event | category | flops | bytes accessed | tf_op | source)
XLA Modules:
  0.0 202.8 jit_solution(16260341085132935242)
XLA Ops:
  2.4 6.4 %all-to-all-start = ((f32[8,40,128]{2,1,0:T(8,128)}), f32[8,40,128]{2,1,0:T(8,128)S(1)}, u32[]{:S(2)}, u32[]{:S(2)}) async-start(f32[8,40,128]{2,1,0:T(8,128)} %pad_maximum_fusion.1), calls=%async_computation | async-start | bytes 327680 | tf_op jit(solution)/shard_map/all_to_all | solution.py:148
  8.8 2.7 %collective-permute-start.1 = (bf16[14,128,128]{2,1,0:T(8,128)(2,1)}, bf16[14,128,128]{2,1,0:T(8,128)(2,1)S(1)}, u32[]{:S(2)}, u32[]{:S(2)}) collective-permute-start(bf16[14,128,128]{2,1,0:T(8,128)(2,1)} %bitcast.18), channel_id=1, source_target_pairs={{0,129},{1,128},{128,0},{129,1},{2,131},{3,130},{130,2},{131,3},{4... | collective-permute-start | bytes 1376264 | tf_op jit(solution)/shard_map/ppermute | solution.py:28
  12.6 1.8 collective-permute-start.10
  14.7 2.2 %collective-permute-start = (f32[8,40,128]{2,1,0:T(8,128)S(1)}, f32[8,40,128]{2,1,0:T(8,128)S(1)}, u32[]{:S(2)}, u32[]{:S(2)}) collective-permute-start(f32[8,40,128]{2,1,0:T(8,128)S(1)} %all-to-all-done), channel_id=1, source_target_pairs={{0,8},{8,0},{1,9},{9,1},{2,10},{10,2},{3,11},{11,3},{4,12},{12,4},... | collective-permute-start | bytes 491528 | tf_op jit(solution)/shard_map/ppermute | solution.py:32
  16.9 1.8 constant_dynamic-update-slice_fusion.19
  20.1 1.9 collective-permute-done.1
  22.0 3.2 %collective-permute-start.2 = (bf16[7,128,128]{2,1,0:T(8,128)(2,1)S(1)}, bf16[7,128,128]{2,1,0:T(8,128)(2,1)S(1)}, u32[]{:S(2)}, u32[]{:S(2)}) collective-permute-start(bf16[7,128,128]{2,1,0:T(8,128)(2,1)S(1)} %slice.38), channel_id=1, source_target_pairs={{0,129},{1,128},{128,0},{129,1},{2,131},{3,130},{130,2},{131,3},{4... | collective-permute-start | bytes 688136 | tf_op jit(solution)/shard_map/ppermute | solution.py:28
  25.3 5.2 %collective-permute-start.20 = (bf16[16,32,128]{2,1,0:T(8,128)(2,1)S(1)}, bf16[16,32,128]{2,1,0:T(8,128)(2,1)S(1)}, u32[]{:S(2)}, u32[]{:S(2)}) collective-permute-start(bf16[16,32,128]{2,1,0:T(8,128)(2,1)S(1)} %fusion.refs_0_), channel_id=1, source_target_pairs={{0,6},{2,0},{4,2},{6,4},{8,104},{10,106},{12,108},{14,110},{32,38}... | collective-permute-start | bytes 393224 | tf_op jit(solution)/shard_map/ppermute | solution.py:45
  30.5 6.6 %list_jobs.1 = (s32[256]{0:T(256)}, s32[1]{0:T(128)}) custom-call(s32[448]{0:T(512)} %reshape.28.meta, s32[5]{0:T(128)} %stack.23.where), custom_call_target="tpu_custom_call" | custom-call | tf_op jit(solution)/shard_map/list_jobs/pallas_call | solution.py:167
  37.3 2.7 %collective-permute-start.6 = (bf16[14,128,128]{2,1,0:T(8,128)(2,1)S(1)}, bf16[14,128,128]{2,1,0:T(8,128)(2,1)S(1)}, u32[]{:S(2)}, u32[]{:S(2)}) collective-permute-start(bf16[14,128,128]{2,1,0:T(8,128)(2,1)S(1)} %collective-permute-done.5), channel_id=1, source_target_pairs={{0,129},{1,128},{128,0},{129,1},{2,131},{3,130},{130,2},{131,3},{4... | collective-permute-start | bytes 1376264 | tf_op jit(solution)/shard_map/ppermute | solution.py:28
  41.5 4.6 %collective-permute-done.4 = bf16[7,128,128]{2,1,0:T(8,128)(2,1)S(1)} collective-permute-done((bf16[7,128,128]{2,1,0:T(8,128)(2,1)S(1)}, bf16[7,128,128]{2,1,0:T(8,128)(2,1)S(1)}, u32[]{:S(2)}, u32[]{:S(2)}) %collective-permute-start.4) | collective-permute-done | bytes 229408 | tf_op jit(solution)/shard_map/ppermute | solution.py:28
  51.3 1.8 collective-permute-done.7
  53.1 1.5 collective-permute-start.11
  55.4 2.7 %collective-permute-done.8 = bf16[7,128,128]{2,1,0:T(8,128)(2,1)S(1)} collective-permute-done((bf16[7,128,128]{2,1,0:T(8,128)(2,1)S(1)}, bf16[7,128,128]{2,1,0:T(8,128)(2,1)S(1)}, u32[]{:S(2)}, u32[]{:S(2)}) %collective-permute-start.8) | collective-permute-done | bytes 229408 | tf_op jit(solution)/shard_map/ppermute | solution.py:32
  63.9 2.8 %collective-permute-start.21 = (bf16[16,32,128]{2,1,0:T(8,128)(2,1)S(1)}, bf16[16,32,128]{2,1,0:T(8,128)(2,1)S(1)}, u32[]{:S(2)}, u32[]{:S(2)}) collective-permute-start(bf16[16,32,128]{2,1,0:T(8,128)(2,1)S(1)} %fusion.refs_0_), channel_id=1, source_target_pairs={{0,4},{2,6},{4,0},{6,2},{8,72},{10,74},{12,76},{14,78},{32,36},{34... | collective-permute-start | bytes 393224 | tf_op jit(solution)/shard_map/ppermute | solution.py:45
  73.7 3.1 %collective-permute-done.22.refs_3_ = bf16[16,32,128]{2,1,0:T(8,128)(2,1)S(1)} collective-permute-done((bf16[16,32,128]{2,1,0:T(8,128)(2,1)S(1)}, bf16[16,32,128]{2,1,0:T(8,128)(2,1)S(1)}, u32[]{:S(2)}, u32[]{:S(2)}) %collective-permute-start.22) | collective-permute-done | bytes 131104 | tf_op jit(solution)/shard_map/ppermute | solution.py:45
  76.8 3.1 %copy-done = bf16[224,128,128]{2,1,0:T(8,128)(2,1)S(1)} copy-done((bf16[224,128,128]{2,1,0:T(8,128)(2,1)S(1)}, bf16[224,128,128]{2,1,0:T(8,128)(2,1)}, u32[]{:S(2)}) %copy-start) | copy-done | bytes 7340056
  79.9 4.8 %apply_tiles.4 = (f32[16,32,128]{2,1,0:T(8,128)S(1)}, bf16[16,32,128]{2,1,0:T(8,128)(2,1)S(1)}, bf16[16,32,128]{2,1,0:T(8,128)(2,1)S(1)}, bf16[16,32,128]{2,1,0:T(8,128)(2,1)S(1)}) custom-call(s32[256]{0:T(256)S(1)} %copy-done.5, s32[1]{0:T(128)} %get-tuple-element.24.count, s32[5]{0:T(128)S(1)} %copy-done.4, bf16[224,128,128]{2,1,0:T(8,128)(2,1)S(1)} %copy-done, ...), custom_call_target="tpu_custom_call" | custom-call | tf_op jit(solution)/shard_map/apply_tiles/pallas_call | solution.py:194
  86.2 2.4 %collective-permute-start.25 = (bf16[16,32,128]{2,1,0:T(8,128)(2,1)S(1)}, bf16[16,32,128]{2,1,0:T(8,128)(2,1)S(1)}, u32[]{:S(2)}, u32[]{:S(2)}) collective-permute-start(bf16[16,32,128]{2,1,0:T(8,128)(2,1)S(1)} %get-tuple-element.28), channel_id=1, source_target_pairs={{0,96},{2,98},{4,100},{6,102},{8,14},{10,8},{12,10},{14,12},{32,0}... | collective-permute-start | bytes 393224 | tf_op jit(solution)/shard_map/ppermute | solution.py:45
  88.6 1.6 collective-permute-done.23
  90.2 1.6 collective-permute-done.24
  91.9 4.5 %collective-permute-start.26 = (f32[16,32,128]{2,1,0:T(8,128)S(1)}, f32[16,32,128]{2,1,0:T(8,128)S(1)}, u32[]{:S(2)}, u32[]{:S(2)}) collective-permute-start(f32[16,32,128]{2,1,0:T(8,128)S(1)} %convert_add_fusion.3), channel_id=1, source_target_pairs={{0,8},{8,0},{1,9},{9,1},{2,10},{10,2},{3,11},{11,3},{4,12},{12,4},... | collective-permute-start | bytes 786440 | tf_op jit(solution)/shard_map/ppermute | solution.py:32
  100.4 3.0 %collective-permute-start.27 = (bf16[16,32,128]{2,1,0:T(8,128)(2,1)S(1)}, bf16[16,32,128]{2,1,0:T(8,128)(2,1)S(1)}, u32[]{:S(2)}, u32[]{:S(2)}) collective-permute-start(bf16[16,32,128]{2,1,0:T(8,128)(2,1)S(1)} %get-tuple-element.45.refs_0_), channel_id=1, source_target_pairs={{0,6},{2,0},{4,2},{6,4},{8,104},{10,106},{12,108},{14,110},{32,38}... | collective-permute-start | bytes 393224 | tf_op jit(solution)/shard_map/ppermute | solution.py:45
  103.4 3.0 %collective-permute-start.28 = (bf16[16,32,128]{2,1,0:T(8,128)(2,1)S(1)}, bf16[16,32,128]{2,1,0:T(8,128)(2,1)S(1)}, u32[]{:S(2)}, u32[]{:S(2)}) collective-permute-start(bf16[16,32,128]{2,1,0:T(8,128)(2,1)S(1)} %get-tuple-element.45.refs_0_), channel_id=1, source_target_pairs={{0,4},{2,6},{4,0},{6,2},{8,72},{10,74},{12,76},{14,78},{32,36},{34... | collective-permute-start | bytes 393224 | tf_op jit(solution)/shard_map/ppermute | solution.py:45
  106.4 2.7 %collective-permute-done.27.refs_1_ = bf16[16,32,128]{2,1,0:T(8,128)(2,1)S(1)} collective-permute-done((bf16[16,32,128]{2,1,0:T(8,128)(2,1)S(1)}, bf16[16,32,128]{2,1,0:T(8,128)(2,1)S(1)}, u32[]{:S(2)}, u32[]{:S(2)}) %collective-permute-start.27) | collective-permute-done | bytes 131104 | tf_op jit(solution)/shard_map/ppermute | solution.py:45
  109.1 4.6 %collective-permute-done.28.refs_2_ = bf16[16,32,128]{2,1,0:T(8,128)(2,1)S(1)} collective-permute-done((bf16[16,32,128]{2,1,0:T(8,128)(2,1)S(1)}, bf16[16,32,128]{2,1,0:T(8,128)(2,1)S(1)}, u32[]{:S(2)}, u32[]{:S(2)}) %collective-permute-start.28) | collective-permute-done | bytes 131104 | tf_op jit(solution)/shard_map/ppermute | solution.py:45
  114.0 3.1 %copy-done.1 = bf16[224,128,128]{2,1,0:T(8,128)(2,1)S(1)} copy-done((bf16[224,128,128]{2,1,0:T(8,128)(2,1)S(1)}, bf16[224,128,128]{2,1,0:T(8,128)(2,1)}, u32[]{:S(2)}) %copy-start.1) | copy-done | bytes 7340056
  117.1 4.8 %apply_tiles.5 = (f32[16,32,128]{2,1,0:T(8,128)S(1)}, bf16[16,32,128]{2,1,0:T(8,128)(2,1)S(1)}, bf16[16,32,128]{2,1,0:T(8,128)(2,1)S(1)}, bf16[16,32,128]{2,1,0:T(8,128)(2,1)S(1)}) custom-call(s32[256]{0:T(256)S(1)} %copy-done.5, s32[1]{0:T(128)} %get-tuple-element.24.count, s32[5]{0:T(128)S(1)} %copy-done.4, bf16[224,128,128]{2,1,0:T(8,128)(2,1)S(1)} %copy-done.1, ...), custom_call_target="tpu_custom_call" | custom-call | tf_op jit(solution)/shard_map/apply_tiles/pallas_call | solution.py:194
  123.0 1.8 collective-permute-start.32
  124.8 2.9 %collective-permute-done.30 = bf16[16,32,128]{2,1,0:T(8,128)(2,1)S(1)} collective-permute-done((bf16[16,32,128]{2,1,0:T(8,128)(2,1)S(1)}, bf16[16,32,128]{2,1,0:T(8,128)(2,1)S(1)}, u32[]{:S(2)}, u32[]{:S(2)}) %collective-permute-start.30) | collective-permute-done | bytes 131104 | tf_op jit(solution)/shard_map/ppermute | solution.py:45
  130.4 2.7 %collective-permute-start.34 = (bf16[16,32,128]{2,1,0:T(8,128)(2,1)S(1)}, bf16[16,32,128]{2,1,0:T(8,128)(2,1)S(1)}, u32[]{:S(2)}, u32[]{:S(2)}) collective-permute-start(bf16[16,32,128]{2,1,0:T(8,128)(2,1)S(1)} %get-tuple-element.43.refs_0_), channel_id=1, source_target_pairs={{0,6},{2,0},{4,2},{6,4},{8,104},{10,106},{12,108},{14,110},{32,38}... | collective-permute-start | bytes 393224 | tf_op jit(solution)/shard_map/ppermute | solution.py:45
  133.0 2.8 %collective-permute-start.35 = (bf16[16,32,128]{2,1,0:T(8,128)(2,1)S(1)}, bf16[16,32,128]{2,1,0:T(8,128)(2,1)S(1)}, u32[]{:S(2)}, u32[]{:S(2)}) collective-permute-start(bf16[16,32,128]{2,1,0:T(8,128)(2,1)S(1)} %get-tuple-element.43.refs_0_), channel_id=1, source_target_pairs={{0,4},{2,6},{4,0},{6,2},{8,72},{10,74},{12,76},{14,78},{32,36},{34... | collective-permute-start | bytes 393224 | tf_op jit(solution)/shard_map/ppermute | solution.py:45
  136.9 5.6 %collective-permute-done.35.refs_2_ = bf16[16,32,128]{2,1,0:T(8,128)(2,1)S(1)} collective-permute-done((bf16[16,32,128]{2,1,0:T(8,128)(2,1)S(1)}, bf16[16,32,128]{2,1,0:T(8,128)(2,1)S(1)}, u32[]{:S(2)}, u32[]{:S(2)}) %collective-permute-start.35) | collective-permute-done | bytes 131104 | tf_op jit(solution)/shard_map/ppermute | solution.py:45
  143.3 3.1 %copy-done.2 = bf16[224,128,128]{2,1,0:T(8,128)(2,1)S(1)} copy-done((bf16[224,128,128]{2,1,0:T(8,128)(2,1)S(1)}, bf16[224,128,128]{2,1,0:T(8,128)(2,1)}, u32[]{:S(2)}) %copy-start.2) | copy-done | bytes 7340056
  146.3 4.8 %apply_tiles.6 = (f32[16,32,128]{2,1,0:T(8,128)S(1)}, bf16[16,32,128]{2,1,0:T(8,128)(2,1)S(1)}, bf16[16,32,128]{2,1,0:T(8,128)(2,1)S(1)}, bf16[16,32,128]{2,1,0:T(8,128)(2,1)S(1)}) custom-call(s32[256]{0:T(256)S(1)} %copy-done.5, s32[1]{0:T(128)} %get-tuple-element.24.count, s32[5]{0:T(128)S(1)} %copy-done.4, bf16[224,128,128]{2,1,0:T(8,128)(2,1)S(1)} %copy-done.2, ...), custom_call_target="tpu_custom_call" | custom-call | tf_op jit(solution)/shard_map/apply_tiles/pallas_call | solution.py:194
  151.2 1.6 collective-permute-start.37
  152.8 2.7 %collective-permute-start.39 = (bf16[16,32,128]{2,1,0:T(8,128)(2,1)S(1)}, bf16[16,32,128]{2,1,0:T(8,128)(2,1)S(1)}, u32[]{:S(2)}, u32[]{:S(2)}) collective-permute-start(bf16[16,32,128]{2,1,0:T(8,128)(2,1)S(1)} %get-tuple-element.36), channel_id=1, source_target_pairs={{0,96},{2,98},{4,100},{6,102},{8,14},{10,8},{12,10},{14,12},{32,0}... | collective-permute-start | bytes 393224 | tf_op jit(solution)/shard_map/ppermute | solution.py:45
  156.7 1.6 collective-permute-done.38
  158.4 2.1 %collective-permute-start.40 = (f32[16,32,128]{2,1,0:T(8,128)S(1)}, f32[16,32,128]{2,1,0:T(8,128)S(1)}, u32[]{:S(2)}, u32[]{:S(2)}) collective-permute-start(f32[16,32,128]{2,1,0:T(8,128)S(1)} %convert_add_fusion.1), channel_id=1, source_target_pairs={{0,8},{8,0},{1,9},{9,1},{2,10},{10,2},{3,11},{11,3},{4,12},{12,4},... | collective-permute-start | bytes 786440 | tf_op jit(solution)/shard_map/ppermute | solution.py:32
  161.7 3.0 %collective-permute-start.41 = (bf16[16,32,128]{2,1,0:T(8,128)(2,1)S(1)}, bf16[16,32,128]{2,1,0:T(8,128)(2,1)S(1)}, u32[]{:S(2)}, u32[]{:S(2)}) collective-permute-start(bf16[16,32,128]{2,1,0:T(8,128)(2,1)S(1)} %get-tuple-element.41.refs_0_), channel_id=1, source_target_pairs={{0,6},{2,0},{4,2},{6,4},{8,104},{10,106},{12,108},{14,110},{32,38}... | collective-permute-start | bytes 393224 | tf_op jit(solution)/shard_map/ppermute | solution.py:45
  164.7 3.8 %collective-permute-start.42 = (bf16[16,32,128]{2,1,0:T(8,128)(2,1)S(1)}, bf16[16,32,128]{2,1,0:T(8,128)(2,1)S(1)}, u32[]{:S(2)}, u32[]{:S(2)}) collective-permute-start(bf16[16,32,128]{2,1,0:T(8,128)(2,1)S(1)} %get-tuple-element.41.refs_0_), channel_id=1, source_target_pairs={{0,4},{2,6},{4,0},{6,2},{8,72},{10,74},{12,76},{14,78},{32,36},{34... | collective-permute-start | bytes 393224 | tf_op jit(solution)/shard_map/ppermute | solution.py:45
  169.3 4.6 %collective-permute-done.42.refs_2_ = bf16[16,32,128]{2,1,0:T(8,128)(2,1)S(1)} collective-permute-done((bf16[16,32,128]{2,1,0:T(8,128)(2,1)S(1)}, bf16[16,32,128]{2,1,0:T(8,128)(2,1)S(1)}, u32[]{:S(2)}, u32[]{:S(2)}) %collective-permute-start.42) | collective-permute-done | bytes 131104 | tf_op jit(solution)/shard_map/ppermute | solution.py:45
  175.1 3.1 %copy-done.3 = bf16[224,128,128]{2,1,0:T(8,128)(2,1)S(1)} copy-done((bf16[224,128,128]{2,1,0:T(8,128)(2,1)S(1)}, bf16[224,128,128]{2,1,0:T(8,128)(2,1)}, u32[]{:S(2)}) %copy-start.3) | copy-done | bytes 7340056
  178.1 4.8 %apply_tiles.7 = (f32[16,32,128]{2,1,0:T(8,128)S(1)}, bf16[16,32,128]{2,1,0:T(8,128)(2,1)S(1)}, bf16[16,32,128]{2,1,0:T(8,128)(2,1)S(1)}, bf16[16,32,128]{2,1,0:T(8,128)(2,1)S(1)}) custom-call(s32[256]{0:T(256)S(1)} %copy-done.5, s32[1]{0:T(128)} %get-tuple-element.24.count, s32[5]{0:T(128)S(1)} %copy-done.4, bf16[224,128,128]{2,1,0:T(8,128)(2,1)S(1)} %copy-done.3, ...), custom_call_target="tpu_custom_call" | custom-call | tf_op jit(solution)/shard_map/apply_tiles/pallas_call | solution.py:194
  183.0 2.4 %collective-permute-start.44 = (bf16[16,32,128]{2,1,0:T(8,128)(2,1)S(1)}, bf16[16,32,128]{2,1,0:T(8,128)(2,1)S(1)}, u32[]{:S(2)}, u32[]{:S(2)}) collective-permute-start(bf16[16,32,128]{2,1,0:T(8,128)(2,1)S(1)} %get-tuple-element.38), channel_id=1, source_target_pairs={{0,64},{2,66},{4,68},{6,70},{8,12},{10,14},{12,8},{14,10},{32,96},... | collective-permute-start | bytes 393224 | tf_op jit(solution)/shard_map/ppermute | solution.py:45
  185.7 2.4 %collective-permute-start.46 = (bf16[16,32,128]{2,1,0:T(8,128)(2,1)S(1)}, bf16[16,32,128]{2,1,0:T(8,128)(2,1)S(1)}, u32[]{:S(2)}, u32[]{:S(2)}) collective-permute-start(bf16[16,32,128]{2,1,0:T(8,128)(2,1)S(1)} %get-tuple-element.40), channel_id=1, source_target_pairs={{0,96},{2,98},{4,100},{6,102},{8,14},{10,8},{12,10},{14,12},{32,0}... | collective-permute-start | bytes 393224 | tf_op jit(solution)/shard_map/ppermute | solution.py:45
  188.4 2.3 %collective-permute-done.45 = bf16[16,32,128]{2,1,0:T(8,128)(2,1)S(1)} collective-permute-done((bf16[16,32,128]{2,1,0:T(8,128)(2,1)S(1)}, bf16[16,32,128]{2,1,0:T(8,128)(2,1)S(1)}, u32[]{:S(2)}, u32[]{:S(2)}) %collective-permute-start.45) | collective-permute-done | bytes 131104 | tf_op jit(solution)/shard_map/ppermute | solution.py:45
  193.1 9.0 %all_to_all.10 = f32[8,32,128]{2,1,0:T(8,128)S(1)} all-to-all(f32[8,32,128]{2,1,0:T(8,128)S(1)} %slice_select_fusion), channel_id=1, replica_groups=mesh['yl'=2,'zh'=4,'zl'=2,'core'=2,'x'=4,'yh'=2] {'yl','yh','zl'}, dimensions={0} | all-to-all | bytes 262144 | tf_op jit(solution)/shard_map/all_to_all | solution.py:218
  (113 shorter events, 41.6 us)
Async XLA Ops:
  2.4 12.3 %all-to-all-start = ((f32[8,40,128]{2,1,0:T(8,128)}), f32[8,40,128]{2,1,0:T(8,128)S(1)}, u32[]{:S(2)}, u32[]{:S(2)}) async-start(f32[8,40,128]{2,1,0:T(8,128)} %pad_maximum_fusion.1), calls=%async_computation | async-start | bytes 327680 | tf_op jit(solution)/shard_map/all_to_all | solution.py:148
  8.8 13.2 %collective-permute-start.1 = (bf16[14,128,128]{2,1,0:T(8,128)(2,1)}, bf16[14,128,128]{2,1,0:T(8,128)(2,1)S(1)}, u32[]{:S(2)}, u32[]{:S(2)}) collective-permute-start(bf16[14,128,128]{2,1,0:T(8,128)(2,1)} %bitcast.18), channel_id=1, source_target_pairs={{0,129},{1,128},{128,0},{129,1},{2,131},{3,130},{130,2},{131,3},{4... | collective-permute-start | bytes 1376264 | tf_op jit(solution)/shard_map/ppermute | solution.py:28
  11.4 25.7 %collective-permute-start.3 = (bf16[14,128,128]{2,1,0:T(8,128)(2,1)}, bf16[14,128,128]{2,1,0:T(8,128)(2,1)S(1)}, u32[]{:S(2)}, u32[]{:S(2)}) collective-permute-start(bf16[14,128,128]{2,1,0:T(8,128)(2,1)} %bitcast.19), channel_id=1, source_target_pairs={{0,128},{1,129},{128,1},{129,0},{2,130},{3,131},{130,3},{131,2},{4... | collective-permute-start | bytes 1376264 | tf_op jit(solution)/shard_map/ppermute | solution.py:28
  11.4 25.8 %collective-permute-start.5 = (bf16[14,128,128]{2,1,0:T(8,128)(2,1)}, bf16[14,128,128]{2,1,0:T(8,128)(2,1)S(1)}, u32[]{:S(2)}, u32[]{:S(2)}) collective-permute-start(bf16[14,128,128]{2,1,0:T(8,128)(2,1)} %bitcast.20), channel_id=1, source_target_pairs={{0,16},{16,0},{1,17},{17,1},{2,18},{18,2},{3,19},{19,3},{4,20},{20... | collective-permute-start | bytes 1376264 | tf_op jit(solution)/shard_map/ppermute | solution.py:32
  12.6 47.9 %collective-permute-start.10 = (bf16[14,128,128]{2,1,0:T(8,128)(2,1)}, bf16[14,128,128]{2,1,0:T(8,128)(2,1)S(1)}, u32[]{:S(2)}, u32[]{:S(2)}) collective-permute-start(bf16[14,128,128]{2,1,0:T(8,128)(2,1)} %bitcast.21), channel_id=1, source_target_pairs={{0,8},{8,0},{1,9},{9,1},{2,10},{10,2},{3,11},{11,3},{4,12},{12,4},... | collective-permute-start | bytes 1376264 | tf_op jit(solution)/shard_map/ppermute | solution.py:32
  14.7 4.7 %collective-permute-start = (f32[8,40,128]{2,1,0:T(8,128)S(1)}, f32[8,40,128]{2,1,0:T(8,128)S(1)}, u32[]{:S(2)}, u32[]{:S(2)}) collective-permute-start(f32[8,40,128]{2,1,0:T(8,128)S(1)} %all-to-all-done), channel_id=1, source_target_pairs={{0,8},{8,0},{1,9},{9,1},{2,10},{10,2},{3,11},{11,3},{4,12},{12,4},... | collective-permute-start | bytes 491528 | tf_op jit(solution)/shard_map/ppermute | solution.py:32
  22.0 18.7 %collective-permute-start.2 = (bf16[7,128,128]{2,1,0:T(8,128)(2,1)S(1)}, bf16[7,128,128]{2,1,0:T(8,128)(2,1)S(1)}, u32[]{:S(2)}, u32[]{:S(2)}) collective-permute-start(bf16[7,128,128]{2,1,0:T(8,128)(2,1)S(1)} %slice.38), channel_id=1, source_target_pairs={{0,129},{1,128},{128,0},{129,1},{2,131},{3,130},{130,2},{131,3},{4... | collective-permute-start | bytes 688136 | tf_op jit(solution)/shard_map/ppermute | solution.py:28
  25.3 48.4 %collective-permute-start.20 = (bf16[16,32,128]{2,1,0:T(8,128)(2,1)S(1)}, bf16[16,32,128]{2,1,0:T(8,128)(2,1)S(1)}, u32[]{:S(2)}, u32[]{:S(2)}) collective-permute-start(bf16[16,32,128]{2,1,0:T(8,128)(2,1)S(1)} %fusion.refs_0_), channel_id=1, source_target_pairs={{0,6},{2,0},{4,2},{6,4},{8,104},{10,106},{12,108},{14,110},{32,38}... | collective-permute-start | bytes 393224 | tf_op jit(solution)/shard_map/ppermute | solution.py:45
  37.2 8.9 %collective-permute-start.4 = (bf16[7,128,128]{2,1,0:T(8,128)(2,1)S(1)}, bf16[7,128,128]{2,1,0:T(8,128)(2,1)S(1)}, u32[]{:S(2)}, u32[]{:S(2)}) collective-permute-start(bf16[7,128,128]{2,1,0:T(8,128)(2,1)S(1)} %slice.39), channel_id=1, source_target_pairs={{0,128},{1,129},{128,1},{129,0},{2,130},{3,131},{130,3},{131,2},{4... | collective-permute-start | bytes 688136 | tf_op jit(solution)/shard_map/ppermute | solution.py:28
  37.3 12.8 %collective-permute-start.6 = (bf16[14,128,128]{2,1,0:T(8,128)(2,1)S(1)}, bf16[14,128,128]{2,1,0:T(8,128)(2,1)S(1)}, u32[]{:S(2)}, u32[]{:S(2)}) collective-permute-start(bf16[14,128,128]{2,1,0:T(8,128)(2,1)S(1)} %collective-permute-done.5), channel_id=1, source_target_pairs={{0,129},{1,128},{128,0},{129,1},{2,131},{3,130},{130,2},{131,3},{4... | collective-permute-start | bytes 1376264 | tf_op jit(solution)/shard_map/ppermute | solution.py:28
  40.8 19.0 %collective-permute-start.9 = (bf16[14,128,128]{2,1,0:T(8,128)(2,1)S(1)}, bf16[14,128,128]{2,1,0:T(8,128)(2,1)S(1)}, u32[]{:S(2)}, u32[]{:S(2)}) collective-permute-start(bf16[14,128,128]{2,1,0:T(8,128)(2,1)S(1)} %collective-permute-done.5), channel_id=1, source_target_pairs={{0,128},{1,129},{128,1},{129,0},{2,130},{3,131},{130,3},{131,2},{4... | collective-permute-start | bytes 1376264 | tf_op jit(solution)/shard_map/ppermute | solution.py:28
  46.1 7.1 %collective-permute-start.7 = (bf16[7,128,128]{2,1,0:T(8,128)(2,1)S(1)}, bf16[7,128,128]{2,1,0:T(8,128)(2,1)S(1)}, u32[]{:S(2)}, u32[]{:S(2)}) collective-permute-start(bf16[7,128,128]{2,1,0:T(8,128)(2,1)S(1)} %collective-permute-done.2), channel_id=1, source_target_pairs={{0,16},{16,0},{1,17},{17,1},{2,18},{18,2},{3,19},{19,3},{4,20},{20... | collective-permute-start | bytes 688136 | tf_op jit(solution)/shard_map/ppermute | solution.py:32
  50.1 7.9 %collective-permute-start.8 = (bf16[7,128,128]{2,1,0:T(8,128)(2,1)S(1)}, bf16[7,128,128]{2,1,0:T(8,128)(2,1)S(1)}, u32[]{:S(2)}, u32[]{:S(2)}) collective-permute-start(bf16[7,128,128]{2,1,0:T(8,128)(2,1)S(1)} %collective-permute-done.4), channel_id=1, source_target_pairs={{0,16},{16,0},{1,17},{17,1},{2,18},{18,2},{3,19},{19,3},{4,20},{20... | collective-permute-start | bytes 688136 | tf_op jit(solution)/shard_map/ppermute | solution.py:32
  53.1 8.7 %collective-permute-start.11 = (bf16[14,128,128]{2,1,0:T(8,128)(2,1)S(1)}, bf16[14,128,128]{2,1,0:T(8,128)(2,1)S(1)}, u32[]{:S(2)}, u32[]{:S(2)}) collective-permute-start(bf16[14,128,128]{2,1,0:T(8,128)(2,1)S(1)} %collective-permute-done.1), channel_id=1, source_target_pairs={{0,8},{8,0},{1,9},{9,1},{2,10},{10,2},{3,11},{11,3},{4,12},{12,4},... | collective-permute-start | bytes 1376264 | tf_op jit(solution)/shard_map/ppermute | solution.py:32
  58.1 9.4 %collective-permute-start.14 = (bf16[14,128,128]{2,1,0:T(8,128)(2,1)S(1)}, bf16[14,128,128]{2,1,0:T(8,128)(2,1)S(1)}, u32[]{:S(2)}, u32[]{:S(2)}) collective-permute-start(bf16[14,128,128]{2,1,0:T(8,128)(2,1)S(1)} %collective-permute-done.3), channel_id=1, source_target_pairs={{0,8},{8,0},{1,9},{9,1},{2,10},{10,2},{3,11},{11,3},{4,12},{12,4},... | collective-permute-start | bytes 1376264 | tf_op jit(solution)/shard_map/ppermute | solution.py:32
  59.7 8.5 %collective-permute-start.15 = (bf16[14,128,128]{2,1,0:T(8,128)(2,1)S(1)}, bf16[14,128,128]{2,1,0:T(8,128)(2,1)S(1)}, u32[]{:S(2)}, u32[]{:S(2)}) collective-permute-start(bf16[14,128,128]{2,1,0:T(8,128)(2,1)S(1)} %collective-permute-done.5), channel_id=1, source_target_pairs={{0,8},{8,0},{1,9},{9,1},{2,10},{10,2},{3,11},{11,3},{4,12},{12,4},... | collective-permute-start | bytes 1376264 | tf_op jit(solution)/shard_map/ppermute | solution.py:32
  60.5 2.2 %collective-permute-start.12 = (bf16[7,128,128]{2,1,0:T(8,128)(2,1)S(1)}, bf16[7,128,128]{2,1,0:T(8,128)(2,1)S(1)}, u32[]{:S(2)}, u32[]{:S(2)}) collective-permute-start(bf16[7,128,128]{2,1,0:T(8,128)(2,1)S(1)} %collective-permute-done.2), channel_id=1, source_target_pairs={{0,8},{8,0},{1,9},{9,1},{2,10},{10,2},{3,11},{11,3},{4,12},{12,4},... | collective-permute-start | bytes 688136 | tf_op jit(solution)/shard_map/ppermute | solution.py:32
  61.9 2.1 %collective-permute-start.13 = (bf16[7,128,128]{2,1,0:T(8,128)(2,1)S(1)}, bf16[7,128,128]{2,1,0:T(8,128)(2,1)S(1)}, u32[]{:S(2)}, u32[]{:S(2)}) collective-permute-start(bf16[7,128,128]{2,1,0:T(8,128)(2,1)S(1)} %collective-permute-done.4), channel_id=1, source_target_pairs={{0,8},{8,0},{1,9},{9,1},{2,10},{10,2},{3,11},{11,3},{4,12},{12,4},... | collective-permute-start | bytes 688136 | tf_op jit(solution)/shard_map/ppermute | solution.py:32
  62.7 6.9 %collective-permute-start.16 = (bf16[14,128,128]{2,1,0:T(8,128)(2,1)S(1)}, bf16[14,128,128]{2,1,0:T(8,128)(2,1)S(1)}, u32[]{:S(2)}, u32[]{:S(2)}) collective-permute-start(bf16[14,128,128]{2,1,0:T(8,128)(2,1)S(1)} %collective-permute-done.6), channel_id=1, source_target_pairs={{0,8},{8,0},{1,9},{9,1},{2,10},{10,2},{3,11},{11,3},{4,12},{12,4},... | collective-permute-start | bytes 1376264 | tf_op jit(solution)/shard_map/ppermute | solution.py:32
  63.9 9.8 %collective-permute-start.21 = (bf16[16,32,128]{2,1,0:T(8,128)(2,1)S(1)}, bf16[16,32,128]{2,1,0:T(8,128)(2,1)S(1)}, u32[]{:S(2)}, u32[]{:S(2)}) collective-permute-start(bf16[16,32,128]{2,1,0:T(8,128)(2,1)S(1)} %fusion.refs_0_), channel_id=1, source_target_pairs={{0,4},{2,6},{4,0},{6,2},{8,72},{10,74},{12,76},{14,78},{32,36},{34... | collective-permute-start | bytes 393224 | tf_op jit(solution)/shard_map/ppermute | solution.py:45
  67.4 3.0 %collective-permute-start.17 = (bf16[7,128,128]{2,1,0:T(8,128)(2,1)S(1)}, bf16[7,128,128]{2,1,0:T(8,128)(2,1)S(1)}, u32[]{:S(2)}, u32[]{:S(2)}) collective-permute-start(bf16[7,128,128]{2,1,0:T(8,128)(2,1)S(1)} %collective-permute-done.7), channel_id=1, source_target_pairs={{0,8},{8,0},{1,9},{9,1},{2,10},{10,2},{3,11},{11,3},{4,12},{12,4},... | collective-permute-start | bytes 688136 | tf_op jit(solution)/shard_map/ppermute | solution.py:32
  68.3 4.6 %collective-permute-start.19 = (bf16[14,128,128]{2,1,0:T(8,128)(2,1)S(1)}, bf16[14,128,128]{2,1,0:T(8,128)(2,1)S(1)}, u32[]{:S(2)}, u32[]{:S(2)}) collective-permute-start(bf16[14,128,128]{2,1,0:T(8,128)(2,1)S(1)} %collective-permute-done.9), channel_id=1, source_target_pairs={{0,8},{8,0},{1,9},{9,1},{2,10},{10,2},{3,11},{11,3},{4,12},{12,4},... | collective-permute-start | bytes 1376264 | tf_op jit(solution)/shard_map/ppermute | solution.py:32
  69.6 2.6 %collective-permute-start.18 = (bf16[7,128,128]{2,1,0:T(8,128)(2,1)S(1)}, bf16[7,128,128]{2,1,0:T(8,128)(2,1)S(1)}, u32[]{:S(2)}, u32[]{:S(2)}) collective-permute-start(bf16[7,128,128]{2,1,0:T(8,128)(2,1)S(1)} %collective-permute-done.8), channel_id=1, source_target_pairs={{0,8},{8,0},{1,9},{9,1},{2,10},{10,2},{3,11},{11,3},{4,12},{12,4},... | collective-permute-start | bytes 688136 | tf_op jit(solution)/shard_map/ppermute | solution.py:32
  70.4 6.4 %collective-permute-start.22 = (bf16[16,32,128]{2,1,0:T(8,128)(2,1)S(1)}, bf16[16,32,128]{2,1,0:T(8,128)(2,1)S(1)}, u32[]{:S(2)}, u32[]{:S(2)}) collective-permute-start(bf16[16,32,128]{2,1,0:T(8,128)(2,1)S(1)} %fusion.refs_0_), channel_id=1, source_target_pairs={{0,2},{2,4},{4,6},{6,0},{8,40},{10,42},{12,44},{14,46},{32,34},{34... | collective-permute-start | bytes 393224 | tf_op jit(solution)/shard_map/ppermute | solution.py:45
  84.7 5.5 %collective-permute-start.23 = (bf16[16,32,128]{2,1,0:T(8,128)(2,1)S(1)}, bf16[16,32,128]{2,1,0:T(8,128)(2,1)S(1)}, u32[]{:S(2)}, u32[]{:S(2)}) collective-permute-start(bf16[16,32,128]{2,1,0:T(8,128)(2,1)S(1)} %get-tuple-element.26), channel_id=1, source_target_pairs={{0,64},{2,66},{4,68},{6,70},{8,12},{10,14},{12,8},{14,10},{32,96},... | collective-permute-start | bytes 393224 | tf_op jit(solution)/shard_map/ppermute | solution.py:45
  85.9 5.9 %collective-permute-start.24 = (bf16[16,32,128]{2,1,0:T(8,128)(2,1)S(1)}, bf16[16,32,128]{2,1,0:T(8,128)(2,1)S(1)}, u32[]{:S(2)}, u32[]{:S(2)}) collective-permute-start(bf16[16,32,128]{2,1,0:T(8,128)(2,1)S(1)} %get-tuple-element.27), channel_id=1, source_target_pairs={{0,32},{2,34},{4,36},{6,38},{8,10},{10,12},{12,14},{14,8},{32,64},... | collective-permute-start | bytes 393224 | tf_op jit(solution)/shard_map/ppermute | solution.py:45
  86.2 5.6 %collective-permute-start.25 = (bf16[16,32,128]{2,1,0:T(8,128)(2,1)S(1)}, bf16[16,32,128]{2,1,0:T(8,128)(2,1)S(1)}, u32[]{:S(2)}, u32[]{:S(2)}) collective-permute-start(bf16[16,32,128]{2,1,0:T(8,128)(2,1)S(1)} %get-tuple-element.28), channel_id=1, source_target_pairs={{0,96},{2,98},{4,100},{6,102},{8,14},{10,8},{12,10},{14,12},{32,0}... | collective-permute-start | bytes 393224 | tf_op jit(solution)/shard_map/ppermute | solution.py:45
  91.9 8.5 %collective-permute-start.26 = (f32[16,32,128]{2,1,0:T(8,128)S(1)}, f32[16,32,128]{2,1,0:T(8,128)S(1)}, u32[]{:S(2)}, u32[]{:S(2)}) collective-permute-start(f32[16,32,128]{2,1,0:T(8,128)S(1)} %convert_add_fusion.3), channel_id=1, source_target_pairs={{0,8},{8,0},{1,9},{9,1},{2,10},{10,2},{3,11},{11,3},{4,12},{12,4},... | collective-permute-start | bytes 786440 | tf_op jit(solution)/shard_map/ppermute | solution.py:32
  100.4 8.7 %collective-permute-start.27 = (bf16[16,32,128]{2,1,0:T(8,128)(2,1)S(1)}, bf16[16,32,128]{2,1,0:T(8,128)(2,1)S(1)}, u32[]{:S(2)}, u32[]{:S(2)}) collective-permute-start(bf16[16,32,128]{2,1,0:T(8,128)(2,1)S(1)} %get-tuple-element.45.refs_0_), channel_id=1, source_target_pairs={{0,6},{2,0},{4,2},{6,4},{8,104},{10,106},{12,108},{14,110},{32,38}... | collective-permute-start | bytes 393224 | tf_op jit(solution)/shard_map/ppermute | solution.py:45
  103.4 10.3 %collective-permute-start.28 = (bf16[16,32,128]{2,1,0:T(8,128)(2,1)S(1)}, bf16[16,32,128]{2,1,0:T(8,128)(2,1)S(1)}, u32[]{:S(2)}, u32[]{:S(2)}) collective-permute-start(bf16[16,32,128]{2,1,0:T(8,128)(2,1)S(1)} %get-tuple-element.45.refs_0_), channel_id=1, source_target_pairs={{0,4},{2,6},{4,0},{6,2},{8,72},{10,74},{12,76},{14,78},{32,36},{34... | collective-permute-start | bytes 393224 | tf_op jit(solution)/shard_map/ppermute | solution.py:45
  106.4 7.6 %collective-permute-start.29 = (bf16[16,32,128]{2,1,0:T(8,128)(2,1)S(1)}, bf16[16,32,128]{2,1,0:T(8,128)(2,1)S(1)}, u32[]{:S(2)}, u32[]{:S(2)}) collective-permute-start(bf16[16,32,128]{2,1,0:T(8,128)(2,1)S(1)} %get-tuple-element.45.refs_0_), channel_id=1, source_target_pairs={{0,2},{2,4},{4,6},{6,0},{8,40},{10,42},{12,44},{14,46},{32,34},{34... | collective-permute-start | bytes 393224 | tf_op jit(solution)/shard_map/ppermute | solution.py:45
  122.0 5.7 %collective-permute-start.30 = (bf16[16,32,128]{2,1,0:T(8,128)(2,1)S(1)}, bf16[16,32,128]{2,1,0:T(8,128)(2,1)S(1)}, u32[]{:S(2)}, u32[]{:S(2)}) collective-permute-start(bf16[16,32,128]{2,1,0:T(8,128)(2,1)S(1)} %get-tuple-element.30), channel_id=1, source_target_pairs={{0,64},{2,66},{4,68},{6,70},{8,12},{10,14},{12,8},{14,10},{32,96},... | collective-permute-start | bytes 393224 | tf_op jit(solution)/shard_map/ppermute | solution.py:45
  122.1 6.5 %collective-permute-start.31 = (bf16[16,32,128]{2,1,0:T(8,128)(2,1)S(1)}, bf16[16,32,128]{2,1,0:T(8,128)(2,1)S(1)}, u32[]{:S(2)}, u32[]{:S(2)}) collective-permute-start(bf16[16,32,128]{2,1,0:T(8,128)(2,1)S(1)} %get-tuple-element.31), channel_id=1, source_target_pairs={{0,32},{2,34},{4,36},{6,38},{8,10},{10,12},{12,14},{14,8},{32,64},... | collective-permute-start | bytes 393224 | tf_op jit(solution)/shard_map/ppermute | solution.py:45
  123.0 5.6 %collective-permute-start.32 = (bf16[16,32,128]{2,1,0:T(8,128)(2,1)S(1)}, bf16[16,32,128]{2,1,0:T(8,128)(2,1)S(1)}, u32[]{:S(2)}, u32[]{:S(2)}) collective-permute-start(bf16[16,32,128]{2,1,0:T(8,128)(2,1)S(1)} %get-tuple-element.32), channel_id=1, source_target_pairs={{0,96},{2,98},{4,100},{6,102},{8,14},{10,8},{12,10},{14,12},{32,0}... | collective-permute-start | bytes 393224 | tf_op jit(solution)/shard_map/ppermute | solution.py:45
  130.4 6.5 %collective-permute-start.34 = (bf16[16,32,128]{2,1,0:T(8,128)(2,1)S(1)}, bf16[16,32,128]{2,1,0:T(8,128)(2,1)S(1)}, u32[]{:S(2)}, u32[]{:S(2)}) collective-permute-start(bf16[16,32,128]{2,1,0:T(8,128)(2,1)S(1)} %get-tuple-element.43.refs_0_), channel_id=1, source_target_pairs={{0,6},{2,0},{4,2},{6,4},{8,104},{10,106},{12,108},{14,110},{32,38}... | collective-permute-start | bytes 393224 | tf_op jit(solution)/shard_map/ppermute | solution.py:45
  133.0 9.4 %collective-permute-start.35 = (bf16[16,32,128]{2,1,0:T(8,128)(2,1)S(1)}, bf16[16,32,128]{2,1,0:T(8,128)(2,1)S(1)}, u32[]{:S(2)}, u32[]{:S(2)}) collective-permute-start(bf16[16,32,128]{2,1,0:T(8,128)(2,1)S(1)} %get-tuple-element.43.refs_0_), channel_id=1, source_target_pairs={{0,4},{2,6},{4,0},{6,2},{8,72},{10,74},{12,76},{14,78},{32,36},{34... | collective-permute-start | bytes 393224 | tf_op jit(solution)/shard_map/ppermute | solution.py:45
  135.9 7.4 %collective-permute-start.36 = (bf16[16,32,128]{2,1,0:T(8,128)(2,1)S(1)}, bf16[16,32,128]{2,1,0:T(8,128)(2,1)S(1)}, u32[]{:S(2)}, u32[]{:S(2)}) collective-permute-start(bf16[16,32,128]{2,1,0:T(8,128)(2,1)S(1)} %get-tuple-element.43.refs_0_), channel_id=1, source_target_pairs={{0,2},{2,4},{4,6},{6,0},{8,40},{10,42},{12,44},{14,46},{32,34},{34... | collective-permute-start | bytes 393224 | tf_op jit(solution)/shard_map/ppermute | solution.py:45
  151.2 5.5 %collective-permute-start.37 = (bf16[16,32,128]{2,1,0:T(8,128)(2,1)S(1)}, bf16[16,32,128]{2,1,0:T(8,128)(2,1)S(1)}, u32[]{:S(2)}, u32[]{:S(2)}) collective-permute-start(bf16[16,32,128]{2,1,0:T(8,128)(2,1)S(1)} %get-tuple-element.34), channel_id=1, source_target_pairs={{0,64},{2,66},{4,68},{6,70},{8,12},{10,14},{12,8},{14,10},{32,96},... | collective-permute-start | bytes 393224 | tf_op jit(solution)/shard_map/ppermute | solution.py:45
  152.8 5.5 %collective-permute-start.38 = (bf16[16,32,128]{2,1,0:T(8,128)(2,1)S(1)}, bf16[16,32,128]{2,1,0:T(8,128)(2,1)S(1)}, u32[]{:S(2)}, u32[]{:S(2)}) collective-permute-start(bf16[16,32,128]{2,1,0:T(8,128)(2,1)S(1)} %get-tuple-element.35), channel_id=1, source_target_pairs={{0,32},{2,34},{4,36},{6,38},{8,10},{10,12},{12,14},{14,8},{32,64},... | collective-permute-start | bytes 393224 | tf_op jit(solution)/shard_map/ppermute | solution.py:45
  152.8 5.5 %collective-permute-start.39 = (bf16[16,32,128]{2,1,0:T(8,128)(2,1)S(1)}, bf16[16,32,128]{2,1,0:T(8,128)(2,1)S(1)}, u32[]{:S(2)}, u32[]{:S(2)}) collective-permute-start(bf16[16,32,128]{2,1,0:T(8,128)(2,1)S(1)} %get-tuple-element.36), channel_id=1, source_target_pairs={{0,96},{2,98},{4,100},{6,102},{8,14},{10,8},{12,10},{14,12},{32,0}... | collective-permute-start | bytes 393224 | tf_op jit(solution)/shard_map/ppermute | solution.py:45
  158.4 3.2 %collective-permute-start.40 = (f32[16,32,128]{2,1,0:T(8,128)S(1)}, f32[16,32,128]{2,1,0:T(8,128)S(1)}, u32[]{:S(2)}, u32[]{:S(2)}) collective-permute-start(f32[16,32,128]{2,1,0:T(8,128)S(1)} %convert_add_fusion.1), channel_id=1, source_target_pairs={{0,8},{8,0},{1,9},{9,1},{2,10},{10,2},{3,11},{11,3},{4,12},{12,4},... | collective-permute-start | bytes 786440 | tf_op jit(solution)/shard_map/ppermute | solution.py:32
  161.7 7.5 %collective-permute-start.41 = (bf16[16,32,128]{2,1,0:T(8,128)(2,1)S(1)}, bf16[16,32,128]{2,1,0:T(8,128)(2,1)S(1)}, u32[]{:S(2)}, u32[]{:S(2)}) collective-permute-start(bf16[16,32,128]{2,1,0:T(8,128)(2,1)S(1)} %get-tuple-element.41.refs_0_), channel_id=1, source_target_pairs={{0,6},{2,0},{4,2},{6,4},{8,104},{10,106},{12,108},{14,110},{32,38}... | collective-permute-start | bytes 393224 | tf_op jit(solution)/shard_map/ppermute | solution.py:45
  164.7 9.2 %collective-permute-start.42 = (bf16[16,32,128]{2,1,0:T(8,128)(2,1)S(1)}, bf16[16,32,128]{2,1,0:T(8,128)(2,1)S(1)}, u32[]{:S(2)}, u32[]{:S(2)}) collective-permute-start(bf16[16,32,128]{2,1,0:T(8,128)(2,1)S(1)} %get-tuple-element.41.refs_0_), channel_id=1, source_target_pairs={{0,4},{2,6},{4,0},{6,2},{8,72},{10,74},{12,76},{14,78},{32,36},{34... | collective-permute-start | bytes 393224 | tf_op jit(solution)/shard_map/ppermute | solution.py:45
  168.5 6.6 %collective-permute-start.43 = (bf16[16,32,128]{2,1,0:T(8,128)(2,1)S(1)}, bf16[16,32,128]{2,1,0:T(8,128)(2,1)S(1)}, u32[]{:S(2)}, u32[]{:S(2)}) collective-permute-start(bf16[16,32,128]{2,1,0:T(8,128)(2,1)S(1)} %get-tuple-element.41.refs_0_), channel_id=1, source_target_pairs={{0,2},{2,4},{4,6},{6,0},{8,40},{10,42},{12,44},{14,46},{32,34},{34... | collective-permute-start | bytes 393224 | tf_op jit(solution)/shard_map/ppermute | solution.py:45
  183.0 5.4 %collective-permute-start.44 = (bf16[16,32,128]{2,1,0:T(8,128)(2,1)S(1)}, bf16[16,32,128]{2,1,0:T(8,128)(2,1)S(1)}, u32[]{:S(2)}, u32[]{:S(2)}) collective-permute-start(bf16[16,32,128]{2,1,0:T(8,128)(2,1)S(1)} %get-tuple-element.38), channel_id=1, source_target_pairs={{0,64},{2,66},{4,68},{6,70},{8,12},{10,14},{12,8},{14,10},{32,96},... | collective-permute-start | bytes 393224 | tf_op jit(solution)/shard_map/ppermute | solution.py:45
  185.4 5.3 %collective-permute-start.45 = (bf16[16,32,128]{2,1,0:T(8,128)(2,1)S(1)}, bf16[16,32,128]{2,1,0:T(8,128)(2,1)S(1)}, u32[]{:S(2)}, u32[]{:S(2)}) collective-permute-start(bf16[16,32,128]{2,1,0:T(8,128)(2,1)S(1)} %get-tuple-element.39), channel_id=1, source_target_pairs={{0,32},{2,34},{4,36},{6,38},{8,10},{10,12},{12,14},{14,8},{32,64},... | collective-permute-start | bytes 393224 | tf_op jit(solution)/shard_map/ppermute | solution.py:45
  185.7 5.0 %collective-permute-start.46 = (bf16[16,32,128]{2,1,0:T(8,128)(2,1)S(1)}, bf16[16,32,128]{2,1,0:T(8,128)(2,1)S(1)}, u32[]{:S(2)}, u32[]{:S(2)}) collective-permute-start(bf16[16,32,128]{2,1,0:T(8,128)(2,1)S(1)} %get-tuple-element.40), channel_id=1, source_target_pairs={{0,96},{2,98},{4,100},{6,102},{8,14},{10,8},{12,10},{14,12},{32,0}... | collective-permute-start | bytes 393224 | tf_op jit(solution)/shard_map/ppermute | solution.py:45
  190.8 2.2 %collective-permute-start.47 = (f32[16,32,128]{2,1,0:T(8,128)S(1)}, f32[16,32,128]{2,1,0:T(8,128)S(1)}, u32[]{:S(2)}, u32[]{:S(2)}) collective-permute-start(f32[16,32,128]{2,1,0:T(8,128)S(1)} %convert_add_fusion), channel_id=1, source_target_pairs={{0,8},{8,0},{1,9},{9,1},{2,10},{10,2},{3,11},{11,3},{4,12},{12,4},... | collective-permute-start | bytes 786440 | tf_op jit(solution)/shard_map/ppermute | solution.py:32
  (8 other events, 142.1 us)

commit v2 on v1

--- a/solution.py
+++ b/solution.py
@@ -17,15 +17,7 @@
 RING = 4
 SUMS = RING * BLOCKS
 LIST = 256
-
-
-def shift_y(array, step):
-    pairs = []
-    for low in range(2):
-        for high in range(2):
-            target = (high * 2 + low - step) % 4
-            pairs.append((low * 2 + high, target % 2 * 2 + target // 2))
-    return lax.ppermute(array, ("yl", "yh"), pairs)
+STAGE = 2
 
 
 def swap(array, axis):
@@ -45,18 +37,13 @@
     return lax.ppermute(array, ("zh", "core", "x"), pairs)
 
 
-def list_kernel(slots, meta, where, jobs, count):
-    core, high, place, along_y, low = (where[i] for i in range(5))
+def list_kernel(slots, meta, where, jobs, marks):
+    core, high, place = (where[i] for i in range(3))
 
     def source(piece, found):
-        core_s = core ^ (piece >> 3)
-        low_s = low ^ ((piece >> 2) & 1)
-        y_s = (along_y + (piece & 3)) & 3
-        block_s = core_s * 8 + ((y_s & 1) * 2 + (y_s >> 1)) * 2 + low_s
-
         def slot(t, found):
-            row = meta[block_s * 2 * slots + t]
-            col = meta[(block_s * 2 + 1) * slots + t]
+            row = meta[piece * 2 * slots + t]
+            col = meta[(piece * 2 + 1) * slots + t]
             spots = []
             for number in (row, col):
                 group, member = number >> 3, number & 7
@@ -73,23 +60,32 @@
             jobs[found] = ((piece * slots + t) << 16) | (taken << 8) | given
             return found + jnp.where(row >= 0, 1, 0)
 
-        return lax.fori_loop(0, slots, slot, found)
+        found = lax.fori_loop(0, slots, slot, found)
+        marks[piece] = found // BATCH
+        return found
 
     found = lax.fori_loop(0, BLOCKS, source, jnp.int32(0))
     for extra in range(BATCH):
         jobs[found + extra] = SUMS
-    count[0] = (found + BATCH - 1) // BATCH
-
-
-def apply_kernel(jobs, count, where, tiles, *refs):
-    taken = refs[:RING]
-    given = refs[RING : 2 * RING]
-    vectors, sums = refs[2 * RING :]
+    marks[BLOCKS - 1] = (found + BATCH - 1) // BATCH
+
+
+def apply_kernel(jobs, marks, where, gathered, *refs):
+    taken, given = refs[:RING], refs[RING : 2 * RING]
+    vectors, sums, tiles, arrived = refs[2 * RING :]
+    chunk = tiles.shape[0] // BLOCKS * STAGE
+    copies = []
+    for k in range(BLOCKS // STAGE):
+        part = pl.ds(k * chunk, chunk)
+        copies.append(
+            pltpu.make_async_copy(gathered.at[part], tiles.at[part], arrived.at[k])
+        )
+        copies[-1].start()
     for d in range(RING):
         vectors[d * BLOCKS : (d + 1) * BLOCKS] = taken[d][...]
     sums[...] = jnp.zeros_like(sums)
 
-    def multiply(contract):
+    def batches(first, last, contract):
         def batch(step, carry):
             products = []
             for k in range(BATCH):
@@ -109,15 +105,22 @@
                 sums[spot] += product
             return carry
 
-        lax.fori_loop(0, count[0], batch, 0)
-
-    @pl.when(where[0] == 0)
-    def _():
-        multiply(0)
-
-    @pl.when(where[0] != 0)
-    def _():
-        multiply(1)
+        lax.fori_loop(first, last, batch, 0)
+
+    first = 0
+    for stage, copy in enumerate(copies):
+        copy.wait()
+        last = marks[stage * STAGE + STAGE - 1]
+
+        @pl.when(where[0] == 0)
+        def _():
+            batches(first, last, 0)
+
+        @pl.when(where[0] != 0)
+        def _():
+            batches(first, last, 1)
+
+        first = last
 
     for d in range(RING):
         given[d][...] = sums[d * BLOCKS : (d + 1) * BLOCKS].astype(given[d].dtype)
@@ -129,9 +132,7 @@
     part = width // CHIPS
     spot = {name: lax.axis_index(name) for name in SIZES}
     core = spot["core"]
-    where = jnp.stack(
-        [core, spot["zh"], spot["x"], spot["yh"] * 2 + spot["yl"], spot["zl"]]
-    ).astype(jnp.int32)
+    where = jnp.stack([core, spot["zh"], spot["x"]]).astype(jnp.int32)
 
     own_tiles = tiles.reshape(slots, size, size)
     places = jnp.concatenate(
@@ -153,22 +154,16 @@
     start = dealt[:, :part]
     meta = dealt[:, part : part + 2, :slots].astype(jnp.int32).reshape(-1)
 
-    half = slots // 2
-    beside = swap(own_tiles, "zl")
-    up, down = shift_y(own_tiles, 1), shift_y(own_tiles, -1)
-    beside_up, beside_down = shift_y(beside, 1), shift_y(beside, -1)
-    over = shift_y(up[:half], 1), shift_y(down[half:], -1)
-    beside_over = swap(over[0], "zl"), swap(over[1], "zl")
-    pieces = [own_tiles, up, *over, down, beside, beside_up, *beside_over, beside_down]
-    all_tiles = jnp.concatenate(pieces + [swap(piece, "core") for piece in pieces])
+    all_tiles = lax.all_gather(own_tiles, ("core",) + GROUP, axis=0, tiled=True)
+    stored_tiles = pltpu.with_memory_space_constraint(all_tiles, pltpu.HBM)
 
     smem = pl.BlockSpec(memory_space=pltpu.SMEM)
     vmem = pl.BlockSpec(memory_space=pltpu.VMEM)
-    jobs, count = pl.pallas_call(
+    jobs, marks = pl.pallas_call(
         functools.partial(list_kernel, slots),
         out_shape=(
             jax.ShapeDtypeStruct((LIST,), jnp.int32),
-            jax.ShapeDtypeStruct((1,), jnp.int32),
+            jax.ShapeDtypeStruct((BLOCKS,), jnp.int32),
         ),
         in_specs=[smem, smem],
         out_specs=(smem, smem),
@@ -178,11 +173,15 @@
         apply_kernel,
         out_shape=[jax.ShapeDtypeStruct((BLOCKS, part, size), jnp.float32)]
         + [jax.ShapeDtypeStruct((BLOCKS, part, size), jnp.bfloat16)] * (RING - 1),
-        in_specs=[smem, smem, smem] + [vmem] * (1 + RING),
+        in_specs=[smem] * 3
+        + [pl.BlockSpec(memory_space=pltpu.HBM)]
+        + [vmem] * RING,
         out_specs=[vmem] * RING,
         scratch_shapes=[
             pltpu.VMEM((SUMS, part, size), jnp.bfloat16),
             pltpu.VMEM((SUMS + 1, part, size), jnp.float32),
+            pltpu.VMEM((BLOCKS * slots, size, size), jnp.bfloat16),
+            pltpu.SemaphoreType.DMA((BLOCKS // STAGE,)),
         ],
         compiler_params=pltpu.CompilerParams(vmem_limit_bytes=32 << 20),
         name="apply_tiles",
@@ -192,7 +191,7 @@
         low = vectors.astype(jnp.bfloat16)
         gathered = {d: exchange(low, -d, 0) for d in (2, 1, 3)}
         total, *partial = apply_tiles(
-            jobs, count, where, all_tiles, low, *(gathered[d] for d in (1, 2, 3))
+            jobs, marks, where, stored_tiles, low, *(gathered[d] for d in (1, 2, 3))
         )
         sent = [exchange(partial[d - 1], d, 1) for d in (2, 1, 3)]
         for piece in sent:

time: 203 us -> 199 us (0.980)
  local copies, waits for them, and re-layouts: 32.6 us -> 5 us
  starting transfers between devices: 76.4 us -> 59.1 us
  between operations: 3.88 us -> 17 us
  waiting for transfers between devices: 52.9 us -> 65 us
  blocking collectives: 8.97 us -> 21 us
  Pallas kernels: 26 us -> 29.2 us
    all_gather x0 -> x1, waiting for transfers between devices: none -> 26.1 us  [local(): all_tiles = lax.all_gather(own_tiles, ('core',) + GROUP, axis=0, tiled=True)]
    unnamed x33 -> x14, local copies, waits for them, and re-layouts: 28 us -> 1.96 us
    all_to_all x0 -> x1, blocking collectives: none -> 12.1 us  [local(): mine = lax.all_to_all(message, GROUP, 0, 0)]
    ppermute x6 -> x0, starting transfers between devices: 8.67 us -> none  [shift_y(): return lax.ppermute(array, ('yl', 'yh'), pairs)]
    ppermute x6 -> x0, waiting for transfers between devices: 7.79 us -> none  [shift_y(): return lax.ppermute(array, ('yl', 'yh'), pairs)]
    all_to_all x1 -> x0, starting transfers between devices: 6.37 us -> none  [local(): mine = lax.all_to_all(message, GROUP, 0, 0)]
    pallas_call x4, Pallas kernels: 19.4 us -> 23.3 us  [apply_matrix(): apply_tiles(jobs, marks, where, stored_tiles, low, *(gathered[d] for d in...]
    ppermute x18 -> x5, waiting for transfers between devices: 7.82 us -> 4.17 us  [swap(): return lax.ppermute(array, axis, [(0, 1), (1, 0)])]
  transfers between devices with their start and end apart: 49 -> 30, of which waited for: 27 -> 23; matrix products, arithmetic and copies ran while one was open for 9% -> 2% of each run, Pallas kernels for 3% -> 3%
where the time goes in v2:
time: 199 us; the launch traced here: 198 us
  waiting for transfers between devices  65 us (33%)
  starting transfers between devices  59.1 us (30%)
  Pallas kernels  29.2 us (15%)
  blocking collectives  21 us (11%)
  between operations  17 us (9%)
  local copies, waits for them, and re-layouts  5 us (3%)
  other arithmetic  2.07 us (1%)
    ppermute x24, starting transfers between devices, exchange(): return lax.ppermute(array, ('zh', 'core', 'x'), pairs)  43.9 us
    ppermute x24, waiting for transfers between devices, exchange(): return lax.ppermute(array, ('zh', 'core', 'x'), pairs)  34 us
    all_gather x1, waiting for transfers between devices, local(): all_tiles = lax.all_gather(own_tiles, ('core',) + GROUP, axis=0, tiled=True)  26.1 us
    pallas_call x4, Pallas kernels, apply_matrix(): apply_tiles(jobs, marks, where, stored_tiles, low, *(gathered[d] for d in...  23.3 us
    ppermute x5, starting transfers between devices, swap(): return lax.ppermute(array, axis, [(0, 1), (1, 0)])  15.2 us
    all_to_all x1, blocking collectives, local(): mine = lax.all_to_all(message, GROUP, 0, 0)  12.1 us
    all_to_all x1, blocking collectives, local(): back = lax.all_to_all(keep, GROUP, 0, 0)  8.95 us
    pallas_call x1, Pallas kernels, local(): pl.pallas_call(functools.partial(list_kernel, slots), out_shape=(jax.Shap...  5.91 us
  transfers between devices with their start and end apart: 30, of which 23 were waited for; matrix products, arithmetic and copies ran while one was open for 2% of the time, Pallas kernels for 3%

profile of v2, /device:TPU:1, one launch (start us, length us, event | category | flops | bytes accessed | tf_op | source)
XLA Modules:
  0.0 198.4 jit_solution(7899953483424850746)
XLA Ops:
  6.5 0.7 all-gather.3.cloned.1.call-update
  7.3 1.0 copy.10
  9.0 12.1 %all_to_all.10 = f32[8,40,128]{2,1,0:T(8,128)S(1)} all-to-all(f32[8,40,128]{2,1,0:T(8,128)S(1)} %pad_maximum_fusion.1), channel_id=1, replica_groups=mesh['yl'=2,'zh'=4,'zl'=2,'core'=2,'x'=4,'yh'=2] {'yl','yh','zl'}, dimensions={0} | all-to-all | bytes 327680 | tf_op jit(solution)/shard_map/all_to_all | solution.py:149
  21.1 2.0 %collective-permute-start = (f32[8,40,128]{2,1,0:T(8,128)S(1)}, f32[8,40,128]{2,1,0:T(8,128)S(1)}, u32[]{:S(2)}, u32[]{:S(2)}) collective-permute-start(f32[8,40,128]{2,1,0:T(8,128)S(1)} %all_to_all.10), channel_id=1, source_target_pairs={{0,8},{8,0},{1,9},{9,1},{2,10},{10,2},{3,11},{11,3},{4,12},{12,4},... | collective-permute-start | bytes 491528 | tf_op jit(solution)/shard_map/ppermute | solution.py:24
  23.1 1.0 collective-permute-done
  24.2 5.2 %collective-permute-start.1 = (bf16[16,32,128]{2,1,0:T(8,128)(2,1)S(1)}, bf16[16,32,128]{2,1,0:T(8,128)(2,1)S(1)}, u32[]{:S(2)}, u32[]{:S(2)}) collective-permute-start(bf16[16,32,128]{2,1,0:T(8,128)(2,1)S(1)} %fusion.refs_0_), channel_id=1, source_target_pairs={{0,6},{2,0},{4,2},{6,4},{8,104},{10,106},{12,108},{14,110},{32,38}... | collective-permute-start | bytes 393224 | tf_op jit(solution)/shard_map/ppermute | solution.py:37
  29.4 1.2 collective-permute-start.2
  30.5 2.1 %collective-permute-start.3 = (bf16[16,32,128]{2,1,0:T(8,128)(2,1)S(1)}, bf16[16,32,128]{2,1,0:T(8,128)(2,1)S(1)}, u32[]{:S(2)}, u32[]{:S(2)}) collective-permute-start(bf16[16,32,128]{2,1,0:T(8,128)(2,1)S(1)} %fusion.refs_0_), channel_id=1, source_target_pairs={{0,2},{2,4},{4,6},{6,0},{8,40},{10,42},{12,44},{14,46},{32,34},{34... | collective-permute-start | bytes 393224 | tf_op jit(solution)/shard_map/ppermute | solution.py:37
  34.0 5.9 %list_jobs.1 = (s32[256]{0:T(256)}, s32[16]{0:T(128)}) custom-call(s32[448]{0:T(512)} %reshape.28.meta, s32[3]{0:T(128)} %pad_add_fusion.where), custom_call_target="tpu_custom_call" | custom-call | tf_op jit(solution)/shard_map/list_jobs/pallas_call | solution.py:162
  39.9 2.6 %collective-permute-done.2.refs_2_ = bf16[16,32,128]{2,1,0:T(8,128)(2,1)S(1)} collective-permute-done((bf16[16,32,128]{2,1,0:T(8,128)(2,1)S(1)}, bf16[16,32,128]{2,1,0:T(8,128)(2,1)S(1)}, u32[]{:S(2)}, u32[]{:S(2)}) %collective-permute-start.2) | collective-permute-done | bytes 131104 | tf_op jit(solution)/shard_map/ppermute | solution.py:37
  42.8 26.1 %all-gather.3.cloned.1.call-done = bf16[1,1,224,128,128]{4,3,1,0,2:T(8,128)(2,1)} async-done(((bf16[1,1,14,128,128]{4,3,1,0,2:T(8,128)(2,1)}), bf16[1,1,224,128,128]{4,3,1,0,2:T(8,128)(2,1)}) %all-gather.3.cloned.1.call-update) | async-done | bytes 7340048 | tf_op jit(solution)/shard_map/all_gather | solution.py:157
  70.8 5.7 %apply_tiles.4 = (f32[16,32,128]{2,1,0:T(8,128)S(1)}, bf16[16,32,128]{2,1,0:T(8,128)(2,1)S(1)}, bf16[16,32,128]{2,1,0:T(8,128)(2,1)S(1)}, bf16[16,32,128]{2,1,0:T(8,128)(2,1)S(1)}) custom-call(s32[256]{0:T(256)S(1)} %copy-done.2, s32[16]{0:T(128)S(1)} %copy-done.4, s32[3]{0:T(128)S(1)} %copy-done, bf16[224,128,128]{2,1,0:T(8,128)(2,1)} %bitcast.14, ...), custom_call_target="tpu_custom_call" | custom-call | tf_op jit(solution)/shard_map/apply_tiles/pallas_call | solution.py:193
  76.6 2.6 %collective-permute-start.4 = (bf16[16,32,128]{2,1,0:T(8,128)(2,1)S(1)}, bf16[16,32,128]{2,1,0:T(8,128)(2,1)S(1)}, u32[]{:S(2)}, u32[]{:S(2)}) collective-permute-start(bf16[16,32,128]{2,1,0:T(8,128)(2,1)S(1)} %get-tuple-element.26), channel_id=1, source_target_pairs={{0,64},{2,66},{4,68},{6,70},{8,12},{10,14},{12,8},{14,10},{32,96},... | collective-permute-start | bytes 393224 | tf_op jit(solution)/shard_map/ppermute | solution.py:37
  79.1 2.7 %collective-permute-start.6 = (bf16[16,32,128]{2,1,0:T(8,128)(2,1)S(1)}, bf16[16,32,128]{2,1,0:T(8,128)(2,1)S(1)}, u32[]{:S(2)}, u32[]{:S(2)}) collective-permute-start(bf16[16,32,128]{2,1,0:T(8,128)(2,1)S(1)} %get-tuple-element.28), channel_id=1, source_target_pairs={{0,96},{2,98},{4,100},{6,102},{8,14},{10,8},{12,10},{14,12},{32,0}... | collective-permute-start | bytes 393224 | tf_op jit(solution)/shard_map/ppermute | solution.py:37
  82.0 2.5 %collective-permute-done.5 = bf16[16,32,128]{2,1,0:T(8,128)(2,1)S(1)} collective-permute-done((bf16[16,32,128]{2,1,0:T(8,128)(2,1)S(1)}, bf16[16,32,128]{2,1,0:T(8,128)(2,1)S(1)}, u32[]{:S(2)}, u32[]{:S(2)}) %collective-permute-start.5) | collective-permute-done | bytes 131104 | tf_op jit(solution)/shard_map/ppermute | solution.py:37
  84.5 5.1 %collective-permute-start.7 = (f32[16,32,128]{2,1,0:T(8,128)S(1)}, f32[16,32,128]{2,1,0:T(8,128)S(1)}, u32[]{:S(2)}, u32[]{:S(2)}) collective-permute-start(f32[16,32,128]{2,1,0:T(8,128)S(1)} %convert_add_fusion.3), channel_id=1, source_target_pairs={{0,8},{8,0},{1,9},{9,1},{2,10},{10,2},{3,11},{11,3},{4,12},{12,4},... | collective-permute-start | bytes 786440 | tf_op jit(solution)/shard_map/ppermute | solution.py:24
  93.3 1.4 collective-permute-start.10
  94.7 2.2 %collective-permute-start.8 = (bf16[16,32,128]{2,1,0:T(8,128)(2,1)S(1)}, bf16[16,32,128]{2,1,0:T(8,128)(2,1)S(1)}, u32[]{:S(2)}, u32[]{:S(2)}) collective-permute-start(bf16[16,32,128]{2,1,0:T(8,128)(2,1)S(1)} %get-tuple-element.45.refs_0_), channel_id=1, source_target_pairs={{0,6},{2,0},{4,2},{6,4},{8,104},{10,106},{12,108},{14,110},{32,38}... | collective-permute-start | bytes 393224 | tf_op jit(solution)/shard_map/ppermute | solution.py:37
  97.0 3.2 %collective-permute-start.9 = (bf16[16,32,128]{2,1,0:T(8,128)(2,1)S(1)}, bf16[16,32,128]{2,1,0:T(8,128)(2,1)S(1)}, u32[]{:S(2)}, u32[]{:S(2)}) collective-permute-start(bf16[16,32,128]{2,1,0:T(8,128)(2,1)S(1)} %get-tuple-element.45.refs_0_), channel_id=1, source_target_pairs={{0,4},{2,6},{4,0},{6,2},{8,72},{10,74},{12,76},{14,78},{32,36},{34... | collective-permute-start | bytes 393224 | tf_op jit(solution)/shard_map/ppermute | solution.py:37
  101.0 3.8 %collective-permute-done.9.refs_2_ = bf16[16,32,128]{2,1,0:T(8,128)(2,1)S(1)} collective-permute-done((bf16[16,32,128]{2,1,0:T(8,128)(2,1)S(1)}, bf16[16,32,128]{2,1,0:T(8,128)(2,1)S(1)}, u32[]{:S(2)}, u32[]{:S(2)}) %collective-permute-start.9) | collective-permute-done | bytes 131104 | tf_op jit(solution)/shard_map/ppermute | solution.py:37
  104.8 5.9 %apply_tiles.5 = (f32[16,32,128]{2,1,0:T(8,128)S(1)}, bf16[16,32,128]{2,1,0:T(8,128)(2,1)S(1)}, bf16[16,32,128]{2,1,0:T(8,128)(2,1)S(1)}, bf16[16,32,128]{2,1,0:T(8,128)(2,1)S(1)}) custom-call(s32[256]{0:T(256)S(1)} %copy-done.3, s32[16]{0:T(128)S(1)} %copy-done.5, s32[3]{0:T(128)S(1)} %copy-done.1, bf16[224,128,128]{2,1,0:T(8,128)(2,1)} %bitcast.15, ...), custom_call_target="tpu_custom_call" | custom-call | tf_op jit(solution)/shard_map/apply_tiles/pallas_call | solution.py:193
  110.7 3.2 %collective-permute-start.11 = (bf16[16,32,128]{2,1,0:T(8,128)(2,1)S(1)}, bf16[16,32,128]{2,1,0:T(8,128)(2,1)S(1)}, u32[]{:S(2)}, u32[]{:S(2)}) collective-permute-start(bf16[16,32,128]{2,1,0:T(8,128)(2,1)S(1)} %get-tuple-element.30), channel_id=1, source_target_pairs={{0,64},{2,66},{4,68},{6,70},{8,12},{10,14},{12,8},{14,10},{32,96},... | collective-permute-start | bytes 393224 | tf_op jit(solution)/shard_map/ppermute | solution.py:37
  113.9 2.7 %collective-permute-start.13 = (bf16[16,32,128]{2,1,0:T(8,128)(2,1)S(1)}, bf16[16,32,128]{2,1,0:T(8,128)(2,1)S(1)}, u32[]{:S(2)}, u32[]{:S(2)}) collective-permute-start(bf16[16,32,128]{2,1,0:T(8,128)(2,1)S(1)} %get-tuple-element.32), channel_id=1, source_target_pairs={{0,96},{2,98},{4,100},{6,102},{8,14},{10,8},{12,10},{14,12},{32,0}... | collective-permute-start | bytes 393224 | tf_op jit(solution)/shard_map/ppermute | solution.py:37
  116.5 2.6 %collective-permute-done.12 = bf16[16,32,128]{2,1,0:T(8,128)(2,1)S(1)} collective-permute-done((bf16[16,32,128]{2,1,0:T(8,128)(2,1)S(1)}, bf16[16,32,128]{2,1,0:T(8,128)(2,1)S(1)}, u32[]{:S(2)}, u32[]{:S(2)}) %collective-permute-start.12) | collective-permute-done | bytes 131104 | tf_op jit(solution)/shard_map/ppermute | solution.py:37
  119.3 3.1 %collective-permute-start.14 = (f32[16,32,128]{2,1,0:T(8,128)S(1)}, f32[16,32,128]{2,1,0:T(8,128)S(1)}, u32[]{:S(2)}, u32[]{:S(2)}) collective-permute-start(f32[16,32,128]{2,1,0:T(8,128)S(1)} %convert_add_fusion.2), channel_id=1, source_target_pairs={{0,8},{8,0},{1,9},{9,1},{2,10},{10,2},{3,11},{11,3},{4,12},{12,4},... | collective-permute-start | bytes 786440 | tf_op jit(solution)/shard_map/ppermute | solution.py:24
  122.6 1.0 collective-permute-done.14
  123.7 2.4 %collective-permute-start.15 = (bf16[16,32,128]{2,1,0:T(8,128)(2,1)S(1)}, bf16[16,32,128]{2,1,0:T(8,128)(2,1)S(1)}, u32[]{:S(2)}, u32[]{:S(2)}) collective-permute-start(bf16[16,32,128]{2,1,0:T(8,128)(2,1)S(1)} %get-tuple-element.43.refs_0_), channel_id=1, source_target_pairs={{0,6},{2,0},{4,2},{6,4},{8,104},{10,106},{12,108},{14,110},{32,38}... | collective-permute-start | bytes 393224 | tf_op jit(solution)/shard_map/ppermute | solution.py:37
  126.1 2.0 %collective-permute-start.16 = (bf16[16,32,128]{2,1,0:T(8,128)(2,1)S(1)}, bf16[16,32,128]{2,1,0:T(8,128)(2,1)S(1)}, u32[]{:S(2)}, u32[]{:S(2)}) collective-permute-start(bf16[16,32,128]{2,1,0:T(8,128)(2,1)S(1)} %get-tuple-element.43.refs_0_), channel_id=1, source_target_pairs={{0,4},{2,6},{4,0},{6,2},{8,72},{10,74},{12,76},{14,78},{32,36},{34... | collective-permute-start | bytes 393224 | tf_op jit(solution)/shard_map/ppermute | solution.py:37
  128.3 2.5 %collective-permute-done.15.refs_1_ = bf16[16,32,128]{2,1,0:T(8,128)(2,1)S(1)} collective-permute-done((bf16[16,32,128]{2,1,0:T(8,128)(2,1)S(1)}, bf16[16,32,128]{2,1,0:T(8,128)(2,1)S(1)}, u32[]{:S(2)}, u32[]{:S(2)}) %collective-permute-start.15) | collective-permute-done | bytes 131104 | tf_op jit(solution)/shard_map/ppermute | solution.py:37
  130.8 5.0 %collective-permute-done.16.refs_2_ = bf16[16,32,128]{2,1,0:T(8,128)(2,1)S(1)} collective-permute-done((bf16[16,32,128]{2,1,0:T(8,128)(2,1)S(1)}, bf16[16,32,128]{2,1,0:T(8,128)(2,1)S(1)}, u32[]{:S(2)}, u32[]{:S(2)}) %collective-permute-start.16) | collective-permute-done | bytes 131104 | tf_op jit(solution)/shard_map/ppermute | solution.py:37
  136.0 5.7 %apply_tiles.6 = (f32[16,32,128]{2,1,0:T(8,128)S(1)}, bf16[16,32,128]{2,1,0:T(8,128)(2,1)S(1)}, bf16[16,32,128]{2,1,0:T(8,128)(2,1)S(1)}, bf16[16,32,128]{2,1,0:T(8,128)(2,1)S(1)}) custom-call(s32[256]{0:T(256)S(1)} %copy-done.3, s32[16]{0:T(128)S(1)} %copy-done.5, s32[3]{0:T(128)S(1)} %copy-done.1, bf16[224,128,128]{2,1,0:T(8,128)(2,1)} %bitcast.16, ...), custom_call_target="tpu_custom_call" | custom-call | tf_op jit(solution)/shard_map/apply_tiles/pallas_call | solution.py:193
  141.8 2.5 %collective-permute-start.18 = (bf16[16,32,128]{2,1,0:T(8,128)(2,1)S(1)}, bf16[16,32,128]{2,1,0:T(8,128)(2,1)S(1)}, u32[]{:S(2)}, u32[]{:S(2)}) collective-permute-start(bf16[16,32,128]{2,1,0:T(8,128)(2,1)S(1)} %get-tuple-element.34), channel_id=1, source_target_pairs={{0,64},{2,66},{4,68},{6,70},{8,12},{10,14},{12,8},{14,10},{32,96},... | collective-permute-start | bytes 393224 | tf_op jit(solution)/shard_map/ppermute | solution.py:37
  144.3 2.7 %collective-permute-start.20 = (bf16[16,32,128]{2,1,0:T(8,128)(2,1)S(1)}, bf16[16,32,128]{2,1,0:T(8,128)(2,1)S(1)}, u32[]{:S(2)}, u32[]{:S(2)}) collective-permute-start(bf16[16,32,128]{2,1,0:T(8,128)(2,1)S(1)} %get-tuple-element.36), channel_id=1, source_target_pairs={{0,96},{2,98},{4,100},{6,102},{8,14},{10,8},{12,10},{14,12},{32,0}... | collective-permute-start | bytes 393224 | tf_op jit(solution)/shard_map/ppermute | solution.py:37
  147.2 2.4 %collective-permute-done.19 = bf16[16,32,128]{2,1,0:T(8,128)(2,1)S(1)} collective-permute-done((bf16[16,32,128]{2,1,0:T(8,128)(2,1)S(1)}, bf16[16,32,128]{2,1,0:T(8,128)(2,1)S(1)}, u32[]{:S(2)}, u32[]{:S(2)}) %collective-permute-start.19) | collective-permute-done | bytes 131104 | tf_op jit(solution)/shard_map/ppermute | solution.py:37
  149.6 2.1 %collective-permute-start.21 = (f32[16,32,128]{2,1,0:T(8,128)S(1)}, f32[16,32,128]{2,1,0:T(8,128)S(1)}, u32[]{:S(2)}, u32[]{:S(2)}) collective-permute-start(f32[16,32,128]{2,1,0:T(8,128)S(1)} %convert_add_fusion.1), channel_id=1, source_target_pairs={{0,8},{8,0},{1,9},{9,1},{2,10},{10,2},{3,11},{11,3},{4,12},{12,4},... | collective-permute-start | bytes 786440 | tf_op jit(solution)/shard_map/ppermute | solution.py:24
  151.8 1.1 collective-permute-done.21
  153.0 2.1 %collective-permute-start.22 = (bf16[16,32,128]{2,1,0:T(8,128)(2,1)S(1)}, bf16[16,32,128]{2,1,0:T(8,128)(2,1)S(1)}, u32[]{:S(2)}, u32[]{:S(2)}) collective-permute-start(bf16[16,32,128]{2,1,0:T(8,128)(2,1)S(1)} %get-tuple-element.41.refs_0_), channel_id=1, source_target_pairs={{0,6},{2,0},{4,2},{6,4},{8,104},{10,106},{12,108},{14,110},{32,38}... | collective-permute-start | bytes 393224 | tf_op jit(solution)/shard_map/ppermute | solution.py:37
  155.1 2.3 %collective-permute-start.23 = (bf16[16,32,128]{2,1,0:T(8,128)(2,1)S(1)}, bf16[16,32,128]{2,1,0:T(8,128)(2,1)S(1)}, u32[]{:S(2)}, u32[]{:S(2)}) collective-permute-start(bf16[16,32,128]{2,1,0:T(8,128)(2,1)S(1)} %get-tuple-element.41.refs_0_), channel_id=1, source_target_pairs={{0,4},{2,6},{4,0},{6,2},{8,72},{10,74},{12,76},{14,78},{32,36},{34... | collective-permute-start | bytes 393224 | tf_op jit(solution)/shard_map/ppermute | solution.py:37
  157.9 2.2 %collective-permute-done.22.refs_1_ = bf16[16,32,128]{2,1,0:T(8,128)(2,1)S(1)} collective-permute-done((bf16[16,32,128]{2,1,0:T(8,128)(2,1)S(1)}, bf16[16,32,128]{2,1,0:T(8,128)(2,1)S(1)}, u32[]{:S(2)}, u32[]{:S(2)}) %collective-permute-start.22) | collective-permute-done | bytes 131104 | tf_op jit(solution)/shard_map/ppermute | solution.py:37
  160.1 4.5 %collective-permute-done.23.refs_2_ = bf16[16,32,128]{2,1,0:T(8,128)(2,1)S(1)} collective-permute-done((bf16[16,32,128]{2,1,0:T(8,128)(2,1)S(1)}, bf16[16,32,128]{2,1,0:T(8,128)(2,1)S(1)}, u32[]{:S(2)}, u32[]{:S(2)}) %collective-permute-start.23) | collective-permute-done | bytes 131104 | tf_op jit(solution)/shard_map/ppermute | solution.py:37
  164.9 5.9 %apply_tiles.7 = (f32[16,32,128]{2,1,0:T(8,128)S(1)}, bf16[16,32,128]{2,1,0:T(8,128)(2,1)S(1)}, bf16[16,32,128]{2,1,0:T(8,128)(2,1)S(1)}, bf16[16,32,128]{2,1,0:T(8,128)(2,1)S(1)}) custom-call(s32[256]{0:T(256)S(1)} %copy-done.3, s32[16]{0:T(128)S(1)} %copy-done.5, s32[3]{0:T(128)S(1)} %copy-done.1, bf16[224,128,128]{2,1,0:T(8,128)(2,1)} %bitcast.17, ...), custom_call_target="tpu_custom_call" | custom-call | tf_op jit(solution)/shard_map/apply_tiles/pallas_call | solution.py:193
  171.6 2.1 %collective-permute-start.27 = (bf16[16,32,128]{2,1,0:T(8,128)(2,1)S(1)}, bf16[16,32,128]{2,1,0:T(8,128)(2,1)S(1)}, u32[]{:S(2)}, u32[]{:S(2)}) collective-permute-start(bf16[16,32,128]{2,1,0:T(8,128)(2,1)S(1)} %get-tuple-element.40), channel_id=1, source_target_pairs={{0,96},{2,98},{4,100},{6,102},{8,14},{10,8},{12,10},{14,12},{32,0}... | collective-permute-start | bytes 393224 | tf_op jit(solution)/shard_map/ppermute | solution.py:37
  173.7 2.7 %collective-permute-done.25 = bf16[16,32,128]{2,1,0:T(8,128)(2,1)S(1)} collective-permute-done((bf16[16,32,128]{2,1,0:T(8,128)(2,1)S(1)}, bf16[16,32,128]{2,1,0:T(8,128)(2,1)S(1)}, u32[]{:S(2)}, u32[]{:S(2)}) %collective-permute-start.25) | collective-permute-done | bytes 131104 | tf_op jit(solution)/shard_map/ppermute | solution.py:37
  176.4 1.2 collective-permute-done.26
  177.7 2.9 %collective-permute-start.28 = (f32[16,32,128]{2,1,0:T(8,128)S(1)}, f32[16,32,128]{2,1,0:T(8,128)S(1)}, u32[]{:S(2)}, u32[]{:S(2)}) collective-permute-start(f32[16,32,128]{2,1,0:T(8,128)S(1)} %convert_add_fusion), channel_id=1, source_target_pairs={{0,8},{8,0},{1,9},{9,1},{2,10},{10,2},{3,11},{11,3},{4,12},{12,4},... | collective-permute-start | bytes 786440 | tf_op jit(solution)/shard_map/ppermute | solution.py:24
  180.7 1.1 collective-permute-done.28
  181.9 9.0 %all_to_all.11 = f32[8,32,128]{2,1,0:T(8,128)S(1)} all-to-all(f32[8,32,128]{2,1,0:T(8,128)S(1)} %slice_select_fusion), channel_id=1, replica_groups=mesh['yl'=2,'zh'=4,'zl'=2,'core'=2,'x'=4,'yh'=2] {'yl','yh','zl'}, dimensions={0} | all-to-all | bytes 262144 | tf_op jit(solution)/shard_map/all_to_all | solution.py:217
  190.8 0.8 copy.12
  (55 shorter events, 8.8 us)
Async XLA Ops:
  6.5 83.1 %copy-start.6 = (f32[3]{0:T(128)S(1)}, f32[3]{0:T(128)}, u32[]{:S(2)}) copy-start(f32[3]{0:T(128)} %param.9) | copy-start | bytes 40
  6.5 62.3 %all-gather.3.cloned.1.call-start = ((), (), s32[]{:S(2)}) async-start(), calls=%async_computation.2 | async-start | bytes 7798784 | tf_op jit(solution)/shard_map/all_gather | solution.py:157
  21.1 3.0 %collective-permute-start = (f32[8,40,128]{2,1,0:T(8,128)S(1)}, f32[8,40,128]{2,1,0:T(8,128)S(1)}, u32[]{:S(2)}, u32[]{:S(2)}) collective-permute-start(f32[8,40,128]{2,1,0:T(8,128)S(1)} %all_to_all.10), channel_id=1, source_target_pairs={{0,8},{8,0},{1,9},{9,1},{2,10},{10,2},{3,11},{11,3},{4,12},{12,4},... | collective-permute-start | bytes 491528 | tf_op jit(solution)/shard_map/ppermute | solution.py:24
  24.2 15.8 %collective-permute-start.1 = (bf16[16,32,128]{2,1,0:T(8,128)(2,1)S(1)}, bf16[16,32,128]{2,1,0:T(8,128)(2,1)S(1)}, u32[]{:S(2)}, u32[]{:S(2)}) collective-permute-start(bf16[16,32,128]{2,1,0:T(8,128)(2,1)S(1)} %fusion.refs_0_), channel_id=1, source_target_pairs={{0,6},{2,0},{4,2},{6,4},{8,104},{10,106},{12,108},{14,110},{32,38}... | collective-permute-start | bytes 393224 | tf_op jit(solution)/shard_map/ppermute | solution.py:37
  29.4 13.1 %collective-permute-start.2 = (bf16[16,32,128]{2,1,0:T(8,128)(2,1)S(1)}, bf16[16,32,128]{2,1,0:T(8,128)(2,1)S(1)}, u32[]{:S(2)}, u32[]{:S(2)}) collective-permute-start(bf16[16,32,128]{2,1,0:T(8,128)(2,1)S(1)} %fusion.refs_0_), channel_id=1, source_target_pairs={{0,4},{2,6},{4,0},{6,2},{8,72},{10,74},{12,76},{14,78},{32,36},{34... | collective-permute-start | bytes 393224 | tf_op jit(solution)/shard_map/ppermute | solution.py:37
  30.5 12.3 %collective-permute-start.3 = (bf16[16,32,128]{2,1,0:T(8,128)(2,1)S(1)}, bf16[16,32,128]{2,1,0:T(8,128)(2,1)S(1)}, u32[]{:S(2)}, u32[]{:S(2)}) collective-permute-start(bf16[16,32,128]{2,1,0:T(8,128)(2,1)S(1)} %fusion.refs_0_), channel_id=1, source_target_pairs={{0,2},{2,4},{4,6},{6,0},{8,40},{10,42},{12,44},{14,46},{32,34},{34... | collective-permute-start | bytes 393224 | tf_op jit(solution)/shard_map/ppermute | solution.py:37
  33.3 71.5 %copy-start.1 = (s32[3]{0:T(128)S(1)}, s32[3]{0:T(128)}, u32[]{:S(2)}) copy-start(s32[3]{0:T(128)} %pad_add_fusion.where) | copy-start | bytes 40
  39.9 64.9 %copy-start.3 = (s32[256]{0:T(256)S(1)}, s32[256]{0:T(256)}, u32[]{:S(2)}) copy-start(s32[256]{0:T(256)} %get-tuple-element.23.jobs) | copy-start | bytes 3076
  39.9 64.9 %copy-start.5 = (s32[16]{0:T(128)S(1)}, s32[16]{0:T(128)}, u32[]{:S(2)}) copy-start(s32[16]{0:T(128)} %get-tuple-element.24.marks) | copy-start | bytes 196
  68.9 0.7 copy-start
  69.5 0.7 copy-start.2
  70.2 0.6 copy-start.4
  76.6 5.4 %collective-permute-start.4 = (bf16[16,32,128]{2,1,0:T(8,128)(2,1)S(1)}, bf16[16,32,128]{2,1,0:T(8,128)(2,1)S(1)}, u32[]{:S(2)}, u32[]{:S(2)}) collective-permute-start(bf16[16,32,128]{2,1,0:T(8,128)(2,1)S(1)} %get-tuple-element.26), channel_id=1, source_target_pairs={{0,64},{2,66},{4,68},{6,70},{8,12},{10,14},{12,8},{14,10},{32,96},... | collective-permute-start | bytes 393224 | tf_op jit(solution)/shard_map/ppermute | solution.py:37
  79.1 5.3 %collective-permute-start.5 = (bf16[16,32,128]{2,1,0:T(8,128)(2,1)S(1)}, bf16[16,32,128]{2,1,0:T(8,128)(2,1)S(1)}, u32[]{:S(2)}, u32[]{:S(2)}) collective-permute-start(bf16[16,32,128]{2,1,0:T(8,128)(2,1)S(1)} %get-tuple-element.27), channel_id=1, source_target_pairs={{0,32},{2,34},{4,36},{6,38},{8,10},{10,12},{12,14},{14,8},{32,64},... | collective-permute-start | bytes 393224 | tf_op jit(solution)/shard_map/ppermute | solution.py:37
  79.1 5.3 %collective-permute-start.6 = (bf16[16,32,128]{2,1,0:T(8,128)(2,1)S(1)}, bf16[16,32,128]{2,1,0:T(8,128)(2,1)S(1)}, u32[]{:S(2)}, u32[]{:S(2)}) collective-permute-start(bf16[16,32,128]{2,1,0:T(8,128)(2,1)S(1)} %get-tuple-element.28), channel_id=1, source_target_pairs={{0,96},{2,98},{4,100},{6,102},{8,14},{10,8},{12,10},{14,12},{32,0}... | collective-permute-start | bytes 393224 | tf_op jit(solution)/shard_map/ppermute | solution.py:37
  84.5 8.7 %collective-permute-start.7 = (f32[16,32,128]{2,1,0:T(8,128)S(1)}, f32[16,32,128]{2,1,0:T(8,128)S(1)}, u32[]{:S(2)}, u32[]{:S(2)}) collective-permute-start(f32[16,32,128]{2,1,0:T(8,128)S(1)} %convert_add_fusion.3), channel_id=1, source_target_pairs={{0,8},{8,0},{1,9},{9,1},{2,10},{10,2},{3,11},{11,3},{4,12},{12,4},... | collective-permute-start | bytes 786440 | tf_op jit(solution)/shard_map/ppermute | solution.py:24
  93.3 7.1 %collective-permute-start.10 = (bf16[16,32,128]{2,1,0:T(8,128)(2,1)S(1)}, bf16[16,32,128]{2,1,0:T(8,128)(2,1)S(1)}, u32[]{:S(2)}, u32[]{:S(2)}) collective-permute-start(bf16[16,32,128]{2,1,0:T(8,128)(2,1)S(1)} %get-tuple-element.45.refs_0_), channel_id=1, source_target_pairs={{0,2},{2,4},{4,6},{6,0},{8,40},{10,42},{12,44},{14,46},{32,34},{34... | collective-permute-start | bytes 393224 | tf_op jit(solution)/shard_map/ppermute | solution.py:37
  94.7 6.2 %collective-permute-start.8 = (bf16[16,32,128]{2,1,0:T(8,128)(2,1)S(1)}, bf16[16,32,128]{2,1,0:T(8,128)(2,1)S(1)}, u32[]{:S(2)}, u32[]{:S(2)}) collective-permute-start(bf16[16,32,128]{2,1,0:T(8,128)(2,1)S(1)} %get-tuple-element.45.refs_0_), channel_id=1, source_target_pairs={{0,6},{2,0},{4,2},{6,4},{8,104},{10,106},{12,108},{14,110},{32,38}... | collective-permute-start | bytes 393224 | tf_op jit(solution)/shard_map/ppermute | solution.py:37
  97.0 7.8 %collective-permute-start.9 = (bf16[16,32,128]{2,1,0:T(8,128)(2,1)S(1)}, bf16[16,32,128]{2,1,0:T(8,128)(2,1)S(1)}, u32[]{:S(2)}, u32[]{:S(2)}) collective-permute-start(bf16[16,32,128]{2,1,0:T(8,128)(2,1)S(1)} %get-tuple-element.45.refs_0_), channel_id=1, source_target_pairs={{0,4},{2,6},{4,0},{6,2},{8,72},{10,74},{12,76},{14,78},{32,36},{34... | collective-permute-start | bytes 393224 | tf_op jit(solution)/shard_map/ppermute | solution.py:37
  110.7 5.9 %collective-permute-start.11 = (bf16[16,32,128]{2,1,0:T(8,128)(2,1)S(1)}, bf16[16,32,128]{2,1,0:T(8,128)(2,1)S(1)}, u32[]{:S(2)}, u32[]{:S(2)}) collective-permute-start(bf16[16,32,128]{2,1,0:T(8,128)(2,1)S(1)} %get-tuple-element.30), channel_id=1, source_target_pairs={{0,64},{2,66},{4,68},{6,70},{8,12},{10,14},{12,8},{14,10},{32,96},... | collective-permute-start | bytes 393224 | tf_op jit(solution)/shard_map/ppermute | solution.py:37
  113.9 5.3 %collective-permute-start.12 = (bf16[16,32,128]{2,1,0:T(8,128)(2,1)S(1)}, bf16[16,32,128]{2,1,0:T(8,128)(2,1)S(1)}, u32[]{:S(2)}, u32[]{:S(2)}) collective-permute-start(bf16[16,32,128]{2,1,0:T(8,128)(2,1)S(1)} %get-tuple-element.31), channel_id=1, source_target_pairs={{0,32},{2,34},{4,36},{6,38},{8,10},{10,12},{12,14},{14,8},{32,64},... | collective-permute-start | bytes 393224 | tf_op jit(solution)/shard_map/ppermute | solution.py:37
  113.9 5.3 %collective-permute-start.13 = (bf16[16,32,128]{2,1,0:T(8,128)(2,1)S(1)}, bf16[16,32,128]{2,1,0:T(8,128)(2,1)S(1)}, u32[]{:S(2)}, u32[]{:S(2)}) collective-permute-start(bf16[16,32,128]{2,1,0:T(8,128)(2,1)S(1)} %get-tuple-element.32), channel_id=1, source_target_pairs={{0,96},{2,98},{4,100},{6,102},{8,14},{10,8},{12,10},{14,12},{32,0}... | collective-permute-start | bytes 393224 | tf_op jit(solution)/shard_map/ppermute | solution.py:37
  119.3 4.3 %collective-permute-start.14 = (f32[16,32,128]{2,1,0:T(8,128)S(1)}, f32[16,32,128]{2,1,0:T(8,128)S(1)}, u32[]{:S(2)}, u32[]{:S(2)}) collective-permute-start(f32[16,32,128]{2,1,0:T(8,128)S(1)} %convert_add_fusion.2), channel_id=1, source_target_pairs={{0,8},{8,0},{1,9},{9,1},{2,10},{10,2},{3,11},{11,3},{4,12},{12,4},... | collective-permute-start | bytes 786440 | tf_op jit(solution)/shard_map/ppermute | solution.py:24
  123.7 7.1 %collective-permute-start.15 = (bf16[16,32,128]{2,1,0:T(8,128)(2,1)S(1)}, bf16[16,32,128]{2,1,0:T(8,128)(2,1)S(1)}, u32[]{:S(2)}, u32[]{:S(2)}) collective-permute-start(bf16[16,32,128]{2,1,0:T(8,128)(2,1)S(1)} %get-tuple-element.43.refs_0_), channel_id=1, source_target_pairs={{0,6},{2,0},{4,2},{6,4},{8,104},{10,106},{12,108},{14,110},{32,38}... | collective-permute-start | bytes 393224 | tf_op jit(solution)/shard_map/ppermute | solution.py:37
  126.1 9.8 %collective-permute-start.16 = (bf16[16,32,128]{2,1,0:T(8,128)(2,1)S(1)}, bf16[16,32,128]{2,1,0:T(8,128)(2,1)S(1)}, u32[]{:S(2)}, u32[]{:S(2)}) collective-permute-start(bf16[16,32,128]{2,1,0:T(8,128)(2,1)S(1)} %get-tuple-element.43.refs_0_), channel_id=1, source_target_pairs={{0,4},{2,6},{4,0},{6,2},{8,72},{10,74},{12,76},{14,78},{32,36},{34... | collective-permute-start | bytes 393224 | tf_op jit(solution)/shard_map/ppermute | solution.py:37
  128.1 7.9 %collective-permute-start.17 = (bf16[16,32,128]{2,1,0:T(8,128)(2,1)S(1)}, bf16[16,32,128]{2,1,0:T(8,128)(2,1)S(1)}, u32[]{:S(2)}, u32[]{:S(2)}) collective-permute-start(bf16[16,32,128]{2,1,0:T(8,128)(2,1)S(1)} %get-tuple-element.43.refs_0_), channel_id=1, source_target_pairs={{0,2},{2,4},{4,6},{6,0},{8,40},{10,42},{12,44},{14,46},{32,34},{34... | collective-permute-start | bytes 393224 | tf_op jit(solution)/shard_map/ppermute | solution.py:37
  141.8 5.4 %collective-permute-start.18 = (bf16[16,32,128]{2,1,0:T(8,128)(2,1)S(1)}, bf16[16,32,128]{2,1,0:T(8,128)(2,1)S(1)}, u32[]{:S(2)}, u32[]{:S(2)}) collective-permute-start(bf16[16,32,128]{2,1,0:T(8,128)(2,1)S(1)} %get-tuple-element.34), channel_id=1, source_target_pairs={{0,64},{2,66},{4,68},{6,70},{8,12},{10,14},{12,8},{14,10},{32,96},... | collective-permute-start | bytes 393224 | tf_op jit(solution)/shard_map/ppermute | solution.py:37
  144.2 5.3 %collective-permute-start.19 = (bf16[16,32,128]{2,1,0:T(8,128)(2,1)S(1)}, bf16[16,32,128]{2,1,0:T(8,128)(2,1)S(1)}, u32[]{:S(2)}, u32[]{:S(2)}) collective-permute-start(bf16[16,32,128]{2,1,0:T(8,128)(2,1)S(1)} %get-tuple-element.35), channel_id=1, source_target_pairs={{0,32},{2,34},{4,36},{6,38},{8,10},{10,12},{12,14},{14,8},{32,64},... | collective-permute-start | bytes 393224 | tf_op jit(solution)/shard_map/ppermute | solution.py:37
  144.3 5.3 %collective-permute-start.20 = (bf16[16,32,128]{2,1,0:T(8,128)(2,1)S(1)}, bf16[16,32,128]{2,1,0:T(8,128)(2,1)S(1)}, u32[]{:S(2)}, u32[]{:S(2)}) collective-permute-start(bf16[16,32,128]{2,1,0:T(8,128)(2,1)S(1)} %get-tuple-element.36), channel_id=1, source_target_pairs={{0,96},{2,98},{4,100},{6,102},{8,14},{10,8},{12,10},{14,12},{32,0}... | collective-permute-start | bytes 393224 | tf_op jit(solution)/shard_map/ppermute | solution.py:37
  149.6 3.2 %collective-permute-start.21 = (f32[16,32,128]{2,1,0:T(8,128)S(1)}, f32[16,32,128]{2,1,0:T(8,128)S(1)}, u32[]{:S(2)}, u32[]{:S(2)}) collective-permute-start(f32[16,32,128]{2,1,0:T(8,128)S(1)} %convert_add_fusion.1), channel_id=1, source_target_pairs={{0,8},{8,0},{1,9},{9,1},{2,10},{10,2},{3,11},{11,3},{4,12},{12,4},... | collective-permute-start | bytes 786440 | tf_op jit(solution)/shard_map/ppermute | solution.py:24
  153.0 7.1 %collective-permute-start.22 = (bf16[16,32,128]{2,1,0:T(8,128)(2,1)S(1)}, bf16[16,32,128]{2,1,0:T(8,128)(2,1)S(1)}, u32[]{:S(2)}, u32[]{:S(2)}) collective-permute-start(bf16[16,32,128]{2,1,0:T(8,128)(2,1)S(1)} %get-tuple-element.41.refs_0_), channel_id=1, source_target_pairs={{0,6},{2,0},{4,2},{6,4},{8,104},{10,106},{12,108},{14,110},{32,38}... | collective-permute-start | bytes 393224 | tf_op jit(solution)/shard_map/ppermute | solution.py:37
  155.1 9.5 %collective-permute-start.23 = (bf16[16,32,128]{2,1,0:T(8,128)(2,1)S(1)}, bf16[16,32,128]{2,1,0:T(8,128)(2,1)S(1)}, u32[]{:S(2)}, u32[]{:S(2)}) collective-permute-start(bf16[16,32,128]{2,1,0:T(8,128)(2,1)S(1)} %get-tuple-element.41.refs_0_), channel_id=1, source_target_pairs={{0,4},{2,6},{4,0},{6,2},{8,72},{10,74},{12,76},{14,78},{32,36},{34... | collective-permute-start | bytes 393224 | tf_op jit(solution)/shard_map/ppermute | solution.py:37
  157.4 7.5 %collective-permute-start.24 = (bf16[16,32,128]{2,1,0:T(8,128)(2,1)S(1)}, bf16[16,32,128]{2,1,0:T(8,128)(2,1)S(1)}, u32[]{:S(2)}, u32[]{:S(2)}) collective-permute-start(bf16[16,32,128]{2,1,0:T(8,128)(2,1)S(1)} %get-tuple-element.41.refs_0_), channel_id=1, source_target_pairs={{0,2},{2,4},{4,6},{6,0},{8,40},{10,42},{12,44},{14,46},{32,34},{34... | collective-permute-start | bytes 393224 | tf_op jit(solution)/shard_map/ppermute | solution.py:37
  170.8 5.5 %collective-permute-start.25 = (bf16[16,32,128]{2,1,0:T(8,128)(2,1)S(1)}, bf16[16,32,128]{2,1,0:T(8,128)(2,1)S(1)}, u32[]{:S(2)}, u32[]{:S(2)}) collective-permute-start(bf16[16,32,128]{2,1,0:T(8,128)(2,1)S(1)} %get-tuple-element.38), channel_id=1, source_target_pairs={{0,64},{2,66},{4,68},{6,70},{8,12},{10,14},{12,8},{14,10},{32,96},... | collective-permute-start | bytes 393224 | tf_op jit(solution)/shard_map/ppermute | solution.py:37
  170.9 6.7 %collective-permute-start.26 = (bf16[16,32,128]{2,1,0:T(8,128)(2,1)S(1)}, bf16[16,32,128]{2,1,0:T(8,128)(2,1)S(1)}, u32[]{:S(2)}, u32[]{:S(2)}) collective-permute-start(bf16[16,32,128]{2,1,0:T(8,128)(2,1)S(1)} %get-tuple-element.39), channel_id=1, source_target_pairs={{0,32},{2,34},{4,36},{6,38},{8,10},{10,12},{12,14},{14,8},{32,64},... | collective-permute-start | bytes 393224 | tf_op jit(solution)/shard_map/ppermute | solution.py:37
  171.6 6.0 %collective-permute-start.27 = (bf16[16,32,128]{2,1,0:T(8,128)(2,1)S(1)}, bf16[16,32,128]{2,1,0:T(8,128)(2,1)S(1)}, u32[]{:S(2)}, u32[]{:S(2)}) collective-permute-start(bf16[16,32,128]{2,1,0:T(8,128)(2,1)S(1)} %get-tuple-element.40), channel_id=1, source_target_pairs={{0,96},{2,98},{4,100},{6,102},{8,14},{10,8},{12,10},{14,12},{32,0}... | collective-permute-start | bytes 393224 | tf_op jit(solution)/shard_map/ppermute | solution.py:37
  177.7 4.1 %collective-permute-start.28 = (f32[16,32,128]{2,1,0:T(8,128)S(1)}, f32[16,32,128]{2,1,0:T(8,128)S(1)}, u32[]{:S(2)}, u32[]{:S(2)}) collective-permute-start(f32[16,32,128]{2,1,0:T(8,128)S(1)} %convert_add_fusion), channel_id=1, source_target_pairs={{0,8},{8,0},{1,9},{9,1},{2,10},{10,2},{3,11},{11,3},{4,12},{12,4},... | collective-permute-start | bytes 786440 | tf_op jit(solution)/shard_map/ppermute | solution.py:24
Sparse Core Ops, SparseCore 0:
  9.2 59.6 all-gather.2
